TPU v7x, 32 devices: a whole 2x2x4 slice. The times are simulated.
32 devices in a mesh: row: 4 (over y, x), col: 4 (over z), rep: 2 (over core).
Axes of the slice: x: 2, y: 2, z: 4, core: 2. Of those that a mesh axis runs over, the one named last changes fastest.
Arguments:
- patches: bfloat16 [2, 256, 6144], P('rep', 'col', 'row'), may hold values from -6 to 6
- cotangent: bfloat16 [2, 256, 6144], P('rep', 'col', 'row'), may hold values from -6 to 6
- w_in: bfloat16 [6144, 24576], P('row', 'col'), may hold values from -0.078125 to 0.078125
- w_out: bfloat16 [24576, 6144], P('col', 'row'), may hold values from -0.0390625 to 0.0390625
- moment_in: bfloat16 [2, 6144, 24576], P('rep', 'row', 'col'), may hold values from -2 to 2
- moment_out: bfloat16 [2, 24576, 6144], P('rep', 'col', 'row'), may hold values from -2 to 2
Outputs:
- mixed: bfloat16 [2, 256, 6144], P('rep', 'col', 'row')
- tally_in: bfloat16 [6144, 24576], P('row', 'col')
- tally_out: bfloat16 [24576, 6144], P('col', 'row')
All inputs are finite; a program needn't handle non-finite values.
Results may differ from a plain program's by a relative error of at most 0.0055.
Values may be sent and summed in bfloat16 or wider, within the bound.
No kernel may reach another device: no remote copies, remote signals or barrier semaphores. Data moves between devices by JAX's collectives and lax.ppermute only.
A program may use at most 256 MiB of HBM per device.

v0:
```python
import math

import jax
import jax.numpy as jnp
from jax import lax
from jax.sharding import PartitionSpec as P

momentum_decay = 0.9
vote_scale = 0.3


def gelu_value(pre):
    return 0.5 * pre * (1.0 + lax.erf(pre * (1.0 / math.sqrt(2.0))))


def gelu_slope(pre):
    return 0.5 * (1.0 + lax.erf(pre * (1.0 / math.sqrt(2.0)))) + pre * jnp.exp(-0.5 * pre * pre) * (
        1.0 / math.sqrt(2.0 * math.pi)
    )


def shards(patches, cotangent, w_in, w_out, moment_in, moment_out):
    inputs = lax.all_gather(patches[0], "col", axis=0, tiled=True)
    total_rows = inputs.shape[0]
    norm_factor = 1.0 / math.sqrt(total_rows)
    block = inputs
    pre_share = lax.psum_scatter(
        jnp.dot(block, w_in, preferred_element_type=jnp.float32),
        "row",
        scatter_dimension=0,
        tiled=True,
    )
    hidden_share = gelu_value(pre_share).astype(jnp.bfloat16)
    hidden = lax.all_gather(hidden_share, "row", axis=0, tiled=True)
    block = hidden
    mixed = lax.psum_scatter(
        jnp.dot(block, w_out, preferred_element_type=jnp.float32),
        "col",
        scatter_dimension=0,
        tiled=True,
    ).astype(jnp.bfloat16)
    grads = lax.all_gather(cotangent[0], "col", axis=0, tiled=True)
    block = grads
    back_share = lax.psum_scatter(
        lax.dot_general(
            block, w_out, (((1,), (1,)), ((), ())), preferred_element_type=jnp.float32
        ).astype(jnp.bfloat16),
        "row",
        scatter_dimension=0,
        tiled=True,
    ).astype(jnp.float32)
    slope_share = (back_share * gelu_slope(pre_share)).astype(jnp.bfloat16)
    slope = lax.all_gather(slope_share, "row", axis=0, tiled=True)
    grad_first = (
        lax.dot_general(inputs, slope, (((0,), (0,)), ((), ())), preferred_element_type=jnp.float32)
        * norm_factor
    )
    grad_second = (
        lax.dot_general(hidden, grads, (((0,), (0,)), ((), ())), preferred_element_type=jnp.float32)
        * norm_factor
    )
    moved_first = (
        momentum_decay * moment_in[0].astype(jnp.float32) + (1.0 - momentum_decay) * grad_first
    )
    moved_second = (
        momentum_decay * moment_out[0].astype(jnp.float32) + (1.0 - momentum_decay) * grad_second
    )
    vote_first = jnp.tanh(moved_first / vote_scale).astype(jnp.bfloat16)
    vote_second = jnp.tanh(moved_second / vote_scale).astype(jnp.bfloat16)
    tally_first, tally_second = (
        lax.psum(vote_first, "rep").astype(jnp.float32),
        lax.psum(vote_second, "rep").astype(jnp.float32),
    )
    return (mixed[None], tally_first.astype(jnp.bfloat16), tally_second.astype(jnp.bfloat16))


def solution(mesh):
    in_specs = (
        P("rep", "col", "row"),
        P("rep", "col", "row"),
        P("row", "col"),
        P("col", "row"),
        P("rep", "row", "col"),
        P("rep", "col", "row"),
    )
    out_specs = (P("rep", "col", "row"), P("row", "col"), P("col", "row"))
    return jax.shard_map(shards, mesh=mesh, in_specs=in_specs, out_specs=out_specs, check_vma=False)
```

profile of v0, /device:TPU:9, one launch (start us, length us, event | category | flops | bytes accessed | tf_op | source)
XLA Modules:
  0.0 449.1 jit_solution(2310480168816477119)
XLA Ops:
  7.2 0.0 copy-start
  7.2 0.0 reduce-scatter.8.cloned.1.call-start
  7.2 16.7 %all-gather.1 = bf16[1,256,1536]{2,1,0:T(8,128)(2,1)S(1)} all-gather(bf16[1,64,1536]{2,1,0:T(8,128)(2,1)} %param.7), channel_id=3, replica_groups=mesh['row'=4,'col'=4,'rep'=2] {'col'}, dimensions={1}, use_global_device_ids=true | all-gather | bytes 983040 | tf_op jit(solution)/shard_map/all_gather | solution.py:42
  23.9 10.1 %convolution_convert_fusion = bf16[256,6144]{1,0:T(8,128)(2,1)} fusion(bf16[6144,1536]{1,0:T(8,128)(2,1)} %param.9, bf16[1,256,1536]{2,1,0:T(8,128)(2,1)S(1)} %all-gather.1), kind=kOutput, calls=%fused_computation.8 | convolution fusion | flops 4833411072 | bytes 22806528 | tf_op jit(solution)/shard_map/dot_general | solution.py:45
  34.0 0.0 reduce-scatter.8.cloned.1.call-update
  34.1 0.0 reduce-scatter.4.cloned.1.call-start
  34.1 0.0 copy-done
  34.1 16.0 %all-gather = bf16[1,256,1536]{2,1,0:T(8,128)(2,1)S(1)} all-gather(bf16[1,64,1536]{2,1,0:T(8,128)(2,1)S(1)} %copy-done), channel_id=2, replica_groups=mesh['row'=4,'col'=4,'rep'=2] {'col'}, dimensions={1}, use_global_device_ids=true | all-gather | bytes 983040 | tf_op jit(solution)/shard_map/all_gather | solution.py:23
  50.2 13.9 %fusion.15 = f32[256,6144]{1,0:T(8,128)} fusion(bf16[1536,6144]{1,0:T(8,128)(2,1)} %param.8, bf16[1,256,1536]{2,1,0:T(8,128)(2,1)S(1)} %all-gather), kind=kOutput, calls=%fused_computation.21 | convolution fusion | flops 4831838208 | bytes 25952256 | tf_op jit(solution)/shard_map/dot_general | solution.py:28
  64.1 0.0 reduce-scatter.4.cloned.1.call-update
  64.1 0.0 all-gather.5.cloned.1.call-start
  64.1 16.8 %reduce-scatter.8.cloned.1.call-done = bf16[64,6144]{1,0:T(8,128)(2,1)} async-done(((bf16[256,6144]{1,0:T(8,128)(2,1)}), bf16[64,6144]{1,0:T(8,128)(2,1)}) %reduce-scatter.8.cloned.1.call-update) | async-done | bytes 786448 | tf_op jit(solution)/shard_map/reduce_scatter | solution.py:44
  81.0 73.8 %reduce-scatter.4.cloned.1.call-done = f32[64,6144]{1,0:T(8,128)} async-done(((f32[256,6144]{1,0:T(8,128)}), f32[64,6144]{1,0:T(8,128)}) %reduce-scatter.4.cloned.1.call-update) | async-done | bytes 1572880 | tf_op jit(solution)/shard_map/reduce_scatter | solution.py:27
  154.7 3.6 fusion.11
  158.3 0.0 all-gather.5.cloned.1.call-update
  158.3 0.0 all-gather.7.cloned.1.call-start
  158.4 0.5 all-gather.7.cloned.1.call-update
  158.9 0.0 reduce-scatter.6.cloned.1.call-start
  158.9 24.7 %copy.9 = bf16[1,1536,6144]{1,2,0:T(8,128)(2,1)} copy(bf16[1,1536,6144]{2,1,0:T(8,128)(2,1)} %param.10) | data formatting | bytes 37748736 | tf_op args[4]
  183.6 18.9 %all-gather.5.cloned.1.call-done = bf16[256,6144]{1,0:T(8,128)(2,1)} async-done(((bf16[64,6144]{1,0:T(8,128)(2,1)}), bf16[256,6144]{1,0:T(8,128)(2,1)}) %all-gather.5.cloned.1.call-update) | async-done | bytes 3145744 | tf_op jit(solution)/shard_map/all_gather | solution.py:34
  202.5 10.8 %fusion.17 = f32[256,1536]{1,0:T(8,128)} fusion(bf16[256,6144]{1,0:T(8,128)(2,1)} %all-gather.5.cloned.1.call-done, bf16[6144,1536]{1,0:T(8,128)(2,1)} %param.9), kind=kOutput, calls=%fused_computation.24 | convolution fusion | flops 4831838208 | bytes 23592960 | tf_op jit(solution)/shard_map/dot_general | solution.py:37
  213.2 0.0 reduce-scatter.6.cloned.1.call-update
  213.3 0.2 all-reduce.3.cloned.1.call-start
  213.5 19.9 %fusion.2 = bf16[6144,1536]{1,0:T(8,128)(2,1)} fusion(bf16[1,6144,1536]{2,1,0:T(8,128)(2,1)} %param.11, bf16[256,6144]{1,0:T(8,128)(2,1)} %all-gather.5.cloned.1.call-done, bf16[1,256,1536]{2,1,0:T(8,128)(2,1)S(1)} %all-gather.1), kind=kOutput, calls=%fused_computation.3 | convolution fusion | flops 4888461312 | bytes 41680896 | tf_op jit(solution)/shard_map/dot_general | solution.py:59
  233.4 14.8 %all-gather.7.cloned.1.call-done = bf16[256,6144]{1,0:T(8,128)(2,1)} async-done(((bf16[64,6144]{1,0:T(8,128)(2,1)}), bf16[256,6144]{1,0:T(8,128)(2,1)}) %all-gather.7.cloned.1.call-update) | async-done | bytes 3145744 | tf_op jit(solution)/shard_map/all_gather | solution.py:53
  248.2 20.0 %fusion.5 = bf16[1536,6144]{0,1:T(8,128)(2,1)} fusion(bf16[1,1536,6144]{1,2,0:T(8,128)(2,1)} %copy.9, bf16[256,6144]{1,0:T(8,128)(2,1)} %all-gather.7.cloned.1.call-done, bf16[1,256,1536]{2,1,0:T(8,128)(2,1)S(1)} %all-gather), kind=kOutput, calls=%fused_computation.7 | convolution fusion | flops 4888461312 | bytes 41680896 | tf_op jit(solution)/shard_map/dot_general | solution.py:55
  268.2 0.0 all-reduce.3.cloned.1.call-update
  268.2 15.6 %reduce-scatter.6.cloned.1.call-done = f32[64,1536]{1,0:T(8,128)} async-done(((f32[256,1536]{1,0:T(8,128)}), f32[64,1536]{1,0:T(8,128)}) %reduce-scatter.6.cloned.1.call-update) | async-done | bytes 393232 | tf_op jit(solution)/shard_map/reduce_scatter | solution.py:36
  283.8 1.7 convert_bitcast_fusion
  285.5 115.7 %all-reduce.3.cloned.1.call-done = (bf16[1536,6144]{0,1:T(8,128)(2,1)}, bf16[6144,1536]{1,0:T(8,128)(2,1)}) async-done(((bf16[1536,6144]{0,1:T(8,128)(2,1)}, bf16[6144,1536]{1,0:T(8,128)(2,1)}), (bf16[1536,6144]{0,1:T(8,128)(2,1)}, bf16[6144,1536]{1,0:T(8,128)(2,1)})) %all-reduce.3.cloned.1.call-update) | async-done | bytes 37748752 | tf_op jit(solution)/shard_map/psum | solution.py:71
  401.2 24.6 %copy.10 = bf16[1536,6144]{1,0:T(8,128)(2,1)} copy(bf16[1536,6144]{0,1:T(8,128)(2,1)} %get-tuple-element.6) | data formatting | bytes 37748736
  425.8 16.5 %copy.13 = bf16[6144,1536]{1,0:T(8,128)(2,1)} copy(bf16[6144,1536]{1,0:T(8,128)(2,1)} %get-tuple-element.12) | data formatting | bytes 37748736
Async XLA Ops:
  7.2 27.0 %copy-start = (bf16[1,64,1536]{2,1,0:T(8,128)(2,1)S(1)}, bf16[1,64,1536]{2,1,0:T(8,128)(2,1)}, u32[]{:S(2)}) copy-start(bf16[1,64,1536]{2,1,0:T(8,128)(2,1)} %param.6) | copy-start | bytes 589828
  7.2 73.8 %reduce-scatter.8.cloned.1.call-start = ((), (), s32[]{:S(2)}) async-start(), calls=%async_computation.6 | async-start | bytes 3932160 | tf_op jit(solution)/shard_map/reduce_scatter | solution.py:44
  34.1 120.6 %reduce-scatter.4.cloned.1.call-start = ((), (), s32[]{:S(2)}) async-start(), calls=%async_computation.3 | async-start | bytes 7864320 | tf_op jit(solution)/shard_map/reduce_scatter | solution.py:27
  64.1 138.4 %all-gather.5.cloned.1.call-start = ((), (), s32[]{:S(2)}) async-start(), calls=%async_computation.4 | async-start | bytes 3932160 | tf_op jit(solution)/shard_map/all_gather | solution.py:34
  158.3 89.9 %all-gather.7.cloned.1.call-start = ((), (), s32[]{:S(2)}) async-start(), calls=%async_computation.7 | async-start | bytes 3932160 | tf_op jit(solution)/shard_map/all_gather | solution.py:53
  158.9 124.9 %reduce-scatter.6.cloned.1.call-start = ((), (), s32[]{:S(2)}) async-start(), calls=%async_computation.5 | async-start | bytes 1966080 | tf_op jit(solution)/shard_map/reduce_scatter | solution.py:36
  213.3 188.0 %all-reduce.3.cloned.1.call-start = ((), (), s32[]{:S(2)}) async-start(), calls=%async_computation.8 | async-start | bytes 75497472 | tf_op jit(solution)/shard_map/psum | solution.py:71
Sparse Core Ops, SparseCore 0:
  34.2 46.7 reduce-scatter.7
  84.5 70.1 reduce-scatter.3
  158.4 43.9 all-gather.4
  204.1 44.0 all-gather.6
  250.4 33.3 reduce-scatter.5
  286.8 114.3 all-reduce.2
where the time goes:
time: 451 us; the launch traced here: 449 us
  waiting for transfers between devices  256 us (57%)
  matrix products  74.7 us (17%)
  local copies, waits for them, and re-layouts  65.7 us (15%)
  blocking collectives  32.7 us (7%)
  between operations  14.1 us (3%)
  other arithmetic  5.28 us (1%)
    psum x1, waiting for transfers between devices, shards(): lax.psum(vote_first, 'rep').astype(jnp.float32)  116 us
    reduce_scatter x1, waiting for transfers between devices, shards(): lax.psum_scatter(jnp.dot(block, w_in, preferred_element_type=jnp.float32)...  73.8 us
    unnamed x5, local copies, waits for them, and re-layouts  65.7 us
    dot_general x1, matrix products, shards(): lax.dot_general(inputs, slope, (((0,), (0,)), ((), ())), preferred_elemen...  20 us
    dot_general x1, matrix products, shards(): lax.dot_general(hidden, grads, (((0,), (0,)), ((), ())), preferred_elemen...  19.9 us
    all_gather x1, waiting for transfers between devices, shards(): hidden = lax.all_gather(hidden_share, 'row', axis=0, tiled=True)  18.9 us
    reduce_scatter x1, waiting for transfers between devices, shards(): lax.psum_scatter(lax.dot_general(block, w_out, (((1,), (1,)), ((), ())),...  16.8 us
    all_gather x1, blocking collectives, shards(): grads = lax.all_gather(cotangent[0], 'col', axis=0, tiled=True)  16.7 us
  transfers between devices with their start and end apart: 6, of which 6 were waited for; matrix products, arithmetic and copies ran while one was open for 20% of the time, Pallas kernels for 0%

commit v1 on v0

v1 whole, which is shorter than its diff:
```python
import functools
import math

import jax
import jax.numpy as jnp
from jax import lax
from jax.experimental import pallas as pl
from jax.experimental.pallas import tpu as pltpu
from jax.sharding import PartitionSpec as P

momentum_decay = 0.9
vote_scale = 0.3
vmem_bytes = 48 * 2**20
hbm = pl.BlockSpec(memory_space=pl.ANY)


def cost(flops, moved, transcendentals=0):
    return pl.CostEstimate(
        flops=int(flops), bytes_accessed=int(moved), transcendentals=int(transcendentals)
    )


def gelu_value(pre):
    return 0.5 * pre * (1.0 + lax.erf(pre * (1.0 / math.sqrt(2.0))))


def gelu_slope(pre):
    return 0.5 * (1.0 + lax.erf(pre * (1.0 / math.sqrt(2.0)))) + pre * jnp.exp(-0.5 * pre * pre) * (
        1.0 / math.sqrt(2.0 * math.pi)
    )


def shards_plain(patches, cotangent, w_in, w_out, moment_in, moment_out):
    inputs = lax.all_gather(patches[0], "col", axis=0, tiled=True)
    norm_factor = 1.0 / math.sqrt(inputs.shape[0])
    pre_share = lax.psum_scatter(
        jnp.dot(inputs, w_in, preferred_element_type=jnp.float32),
        "row",
        scatter_dimension=0,
        tiled=True,
    )
    hidden = lax.all_gather(
        gelu_value(pre_share).astype(jnp.bfloat16), "row", axis=0, tiled=True
    )
    mixed = lax.psum_scatter(
        jnp.dot(hidden, w_out, preferred_element_type=jnp.float32),
        "col",
        scatter_dimension=0,
        tiled=True,
    ).astype(jnp.bfloat16)
    grads = lax.all_gather(cotangent[0], "col", axis=0, tiled=True)
    back_share = lax.psum_scatter(
        lax.dot_general(
            grads, w_out, (((1,), (1,)), ((), ())), preferred_element_type=jnp.float32
        ).astype(jnp.bfloat16),
        "row",
        scatter_dimension=0,
        tiled=True,
    ).astype(jnp.float32)
    slope_share = (back_share * gelu_slope(pre_share)).astype(jnp.bfloat16)
    slope = lax.all_gather(slope_share, "row", axis=0, tiled=True)

    def votes(moment, left, right):
        grad = norm_factor * lax.dot_general(
            left, right, (((0,), (0,)), ((), ())), preferred_element_type=jnp.float32
        )
        moved = momentum_decay * moment.astype(jnp.float32) + (1.0 - momentum_decay) * grad
        vote = jnp.tanh(moved / vote_scale).astype(jnp.bfloat16)
        return lax.psum(vote, "rep").astype(jnp.float32).astype(jnp.bfloat16)

    return (
        mixed[None],
        votes(moment_in[0], inputs, slope),
        votes(moment_out[0], hidden, grads),
    )


def project_body(transposed, n_tok, idx, *refs):
    toks, w, (send_a, keep_a, send_b, keep_b, whole) = refs[:n_tok], refs[n_tok], refs[-5:]
    step = pl.program_id(0)

    @pl.when(step == 0)
    def _():
        for b, t in enumerate(toks):
            whole[b * t.shape[0] : (b + 1) * t.shape[0]] = t[...]

    contract = ((1,), (1,)) if transposed else ((1,), (0,))
    out = lax.dot_general(
        whole[...], w[...], (contract, ((), ())), preferred_element_type=jnp.float32
    )
    places = (
        (keep_a, 0), (keep_b, 0),
        (send_a, 0), (keep_b, 1),
        (keep_a, 1), (send_b, 0),
        (send_a, 1), (send_b, 1),
    )
    for at, (ref, slot) in enumerate(places):
        @pl.when(step == at)
        def _():
            ref[slot] = out.astype(ref.dtype)


def project(me, toks, w, transposed, n_row, after=()):
    rows = sum(t.shape[0] for t in toks)
    depth = toks[0].shape[1]
    wide = (w.shape[0] if transposed else w.shape[1]) // (2 * n_row)

    def block(s, idx):
        return ((idx[0] ^ (s // 2)) * 2 + s % 2, 0)

    if transposed:
        w_spec = pl.BlockSpec((wide, depth), block)
    else:
        w_spec = pl.BlockSpec((depth, wide), lambda s, idx: block(s, idx)[::-1])
    send = jax.ShapeDtypeStruct((2, rows, wide), jnp.bfloat16)
    keep = jax.ShapeDtypeStruct((2, rows, wide), jnp.float32)
    whole = jax.ShapeDtypeStruct((rows, depth), jnp.bfloat16)
    return pl.pallas_call(
        functools.partial(project_body, transposed, len(toks)),
        grid_spec=pltpu.PrefetchScalarGridSpec(
            num_scalar_prefetch=1,
            grid=(2 * n_row,),
            in_specs=[pl.BlockSpec(t.shape, lambda s, idx: (0, 0)) for t in toks]
            + [w_spec] + [hbm] * len(after),
            out_specs=[pl.BlockSpec(send.shape, lambda s, idx: (0, 0, 0))] * 4
            + [pl.BlockSpec(whole.shape, lambda s, idx: (0, 0))],
        ),
        out_shape=[send, keep, send, keep, whole],
        compiler_params=pltpu.CompilerParams(vmem_limit_bytes=vmem_bytes),
        cost_estimate=cost(2 * rows * w.size, 2 * w.size + 2 * rows * depth + 24 * rows * wide),
        name="project_back" if transposed else "project_pre",
    )(me, *toks, w, *after)


def mix_body(n_half, n_col, n_after, idx, *refs):
    hidden, w = refs[:n_half], refs[n_half]
    out, pack, total = refs[-3:]
    step = pl.program_id(0)
    for at, h in enumerate(hidden):
        @pl.when(step == at)
        def _():
            part = jnp.dot(h[...], w[...], preferred_element_type=jnp.float32)
            total[...] = part if at == 0 else total[...] + part
            if at >= 2:
                pack[at - 2] = h[...]
    @pl.when(step == n_half - 1)
    def _():
        rows = out.shape[1]
        for b in range(n_col):
            out[lax.rem(idx[1] + n_col - b, n_col)] = total[b * rows : (b + 1) * rows]


def half_spec(whole, h):
    if whole.ndim == 3:
        return pl.BlockSpec((None,) + whole.shape[1:], lambda *_: (h, 0, 0))
    return pl.BlockSpec(whole.shape, lambda *_: (0, 0))


def mix(at, halves, w, n_col, after=()):
    rows, wide = halves[0][0].shape[-2:]
    depth = w.shape[1]
    share = rows // n_col
    n_half = len(halves)
    out = jax.ShapeDtypeStruct((n_col, share, depth), jnp.float32)
    pack = jax.ShapeDtypeStruct((n_half - 2, rows, wide), jnp.bfloat16)
    return pl.pallas_call(
        functools.partial(mix_body, n_half, n_col, len(after)),
        grid_spec=pltpu.PrefetchScalarGridSpec(
            num_scalar_prefetch=1,
            grid=(n_half,),
            in_specs=[half_spec(*h) for h in halves]
            + [pl.BlockSpec((wide, depth), lambda s, idx: ((idx[0] ^ (s // 2)) * 2 + s % 2, 0))]
            + [hbm] * len(after),
            out_specs=[pl.BlockSpec(a.shape, lambda s, idx: (0, 0, 0)) for a in (out, pack)],
            scratch_shapes=[pltpu.VMEM((rows, depth), jnp.float32)],
        ),
        out_shape=[out, pack],
        compiler_params=pltpu.CompilerParams(vmem_limit_bytes=vmem_bytes),
        cost_estimate=cost(2 * rows * w.size, 2 * w.size + 4 * rows * w.shape[0] + 4 * rows * depth),
        name="mix",
    )(at, *[h[0] for h in halves], w, *after)


def late_body(keep_a, got_a, keep_b, got_b, *refs):
    out_a, out_b = refs[-2:]
    for keep, got, out in ((keep_a, got_a, out_a), (keep_b, got_b, out_b)):
        out[...] = (keep[...] + got[...].astype(jnp.float32)).astype(jnp.bfloat16)


def late_sums(keep_a, got_a, keep_b, got_b, after):
    _, rows, wide = keep_a.shape
    spec = pl.BlockSpec((None, rows, wide), lambda i: (1, 0, 0))
    out = jax.ShapeDtypeStruct((rows, wide), jnp.bfloat16)
    return pl.pallas_call(
        late_body,
        grid=(1,),
        in_specs=[spec] * 4 + [hbm] * len(after),
        out_specs=[pl.BlockSpec((rows, wide), lambda i: (0, 0))] * 2,
        out_shape=[out, out],
        compiler_params=pltpu.CompilerParams(vmem_limit_bytes=vmem_bytes),
        name="late_sums",
    )(keep_a, got_a, keep_b, got_b, *after)


def sum_of(keep_a, got_a, late_a, keep_b, got_b, late_b):
    return [
        (0, keep_a[...] + got_a[...].astype(jnp.float32) + late_a[...].astype(jnp.float32)),
        (1, keep_b[...] + got_b[...].astype(jnp.float32) + late_b[...].astype(jnp.float32)),
    ]


def hidden_body(*refs):
    tokens, (hidden, pack, steep) = refs[6], refs[-3:]
    wide = hidden.shape[2]
    for h, pre in sum_of(*refs[:6]):
        value = gelu_value(pre).astype(jnp.bfloat16)
        hidden[h] = pack[h] = value
        pack[2 + h] = tokens[:, h * wide : (h + 1) * wide]
        steep[h] = gelu_slope(pre)


def slope_body(*refs):
    tokens, steep, (slope, pack) = refs[6], refs[7], refs[-2:]
    wide = slope.shape[2]
    for h, back in sum_of(*refs[:6]):
        value = (back * steep[h]).astype(jnp.bfloat16)
        slope[h] = pack[h] = value
        pack[2 + h] = tokens[:, h * wide : (h + 1) * wide]


def finish(body, name, kinds, parts, tokens, more=(), after=()):
    _, rows, wide = parts[0].shape
    kept = pl.BlockSpec((None, rows, wide), lambda i: (0, 0, 0))
    late = pl.BlockSpec((rows, wide), lambda i: (0, 0))
    full = pl.BlockSpec((2, rows, wide), lambda i: (0, 0, 0))
    return pl.pallas_call(
        body,
        grid=(1,),
        in_specs=[kept, kept, late] * 2 + [pl.BlockSpec(tokens.shape, lambda i: (0, 0))]
        + [full] * len(more) + [hbm] * len(after),
        out_specs=[pl.BlockSpec((n, rows, wide), lambda i: (0, 0, 0)) for n, _ in kinds],
        out_shape=[jax.ShapeDtypeStruct((n, rows, wide), k) for n, k in kinds],
        compiler_params=pltpu.CompilerParams(vmem_limit_bytes=vmem_bytes),
        name=name,
    )(*parts, tokens, *more, *after)


def forward_body(from_x, from_y, *refs):
    out_a, out_b = refs[-2:]
    out_a[...] = from_x[...]
    out_b[...] = from_y[...]


def forward(from_x, from_y, after):
    _, rows, wide = from_x.shape
    out = jax.ShapeDtypeStruct((rows, wide), jnp.bfloat16)
    return pl.pallas_call(
        forward_body,
        grid=(1,),
        in_specs=[pl.BlockSpec((None, rows, wide), lambda i, h=h: (h, 0, 0)) for h in range(2)]
        + [hbm] * len(after),
        out_specs=[pl.BlockSpec((rows, wide), lambda i: (0, 0))] * 2,
        out_shape=[out, out],
        compiler_params=pltpu.CompilerParams(vmem_limit_bytes=vmem_bytes),
        name="forward",
    )(from_x, from_y, *after)


def vote_of(grad, moment, scale):
    moved = (momentum_decay / vote_scale) * moment.astype(jnp.float32) + scale * grad
    return jnp.tanh(moved).astype(jnp.bfloat16)


def transposed_dot(left, right):
    return lax.dot_general(
        left, right, (((0,), (0,)), ((), ())), preferred_element_type=jnp.float32
    )


def total_of(first, second):
    return first + second


def tally_in_body(scale, idx, x0, x1, s0, s1, m0, m1, *rest):
    out = rest[-1]
    wide = s0.shape[2]
    for h in range(2):
        for c in range(0, wide, wide // 2):
            part = slice(c, c + wide // 2)
            to = slice(h * wide + c, h * wide + c + wide // 2)
            v0 = vote_of(transposed_dot(x0[...], s0[h, :, part]), m0[:, to], scale)
            v1 = vote_of(transposed_dot(x1[...], s1[h, :, part]), m1[:, to], scale)
            out[:, to] = total_of(v0, v1)


def tally_out_body(scale, idx, c0, c1, s0, s1, m0, m1, *rest):
    out = rest[-1]
    half = c1.shape[2]
    step = half // 2 if half % 256 == 0 else half
    for h in range(2):
        for c in range(0, half, step):
            part = slice(c, c + step)
            to = slice(h * half + c, h * half + c + step)
            v0 = vote_of(transposed_dot(s0[...], c0[:, to]), m0[:, to], scale)
            v1 = vote_of(transposed_dot(s1[...], c1[h, :, part]), m1[:, to], scale)
            out[:, to] = total_of(v0, v1)


def tally(kind, quarters, fixed, halves, moments, into, scale, after=()):
    rows, cols = moments[0].shape
    n_half, (_, toks, wide) = 2 * (quarters.size - 1), halves[0].shape
    if kind == "in":
        high = 256 if wide % 256 == 0 else wide
        grid = (n_half // 2, rows // high)
        per = wide // high
        fixed_specs = [
            pl.BlockSpec((toks, high), lambda k, i, q: (0, i)),
            pl.BlockSpec((None, toks, high), lambda k, i, q: (2 + i // per, 0, i % per)),
        ]
        pair_spec = pl.BlockSpec((2, toks, wide), lambda k, i, q: (k, 0, 0))
        m_spec = pl.BlockSpec((high, 2 * wide), lambda k, i, q: (i, q[k]))
        peer_spec = pl.BlockSpec((None, high, 2 * wide), lambda k, i, q: (q[n_half // 2], i, q[k]))
        body = functools.partial(tally_in_body, scale)
        area = rows * n_half * wide
    else:
        high = 256 if wide % 256 == 0 else wide
        per = wide // high
        grid = (n_half // 2, 2, per)
        fixed_specs = [
            pl.BlockSpec((toks, cols), lambda k, h, i, q: (0, 0)),
            pl.BlockSpec((2, toks, wide), lambda k, h, i, q: (1, 0, 0)),
        ]
        pair_spec = pl.BlockSpec((None, toks, high), lambda k, h, i, q: (2 * k + h, 0, i))
        m_spec = pl.BlockSpec((high, cols), lambda k, h, i, q: ((2 * q[k] + h) * per + i, 0))
        peer_spec = pl.BlockSpec(
            (None, high, cols), lambda k, h, i, q: (q[n_half // 2], (2 * q[k] + h) * per + i, 0)
        )
        body = functools.partial(tally_out_body, scale)
        area = cols * n_half * wide
    old = [] if into is None else [into]
    return pl.pallas_call(
        body,
        grid_spec=pltpu.PrefetchScalarGridSpec(
            num_scalar_prefetch=1,
            grid=grid,
            in_specs=fixed_specs + [pair_spec] * 2
            + [m_spec, peer_spec if moments[1].ndim == 3 else m_spec]
            + [hbm] * len(old + list(after)),
            out_specs=m_spec,
        ),
        out_shape=jax.ShapeDtypeStruct((rows, cols), jnp.bfloat16),
        input_output_aliases={7: 0} if old else {},
        compiler_params=pltpu.CompilerParams(vmem_limit_bytes=vmem_bytes),
        cost_estimate=cost(4 * toks * area, 6 * area, 2 * area),
        name="tally_" + kind,
    )(quarters, *fixed, *halves, *moments, *old, *after)


def shards_square(n_col, n_rep, patches, cotangent, w_in, w_out, moment_in, moment_out):
    n_row = 4
    across_x = [(i, i ^ 1) for i in range(n_row)]
    across_y = [(i, i ^ 2) for i in range(n_row)]
    swap = [(0, 1), (1, 0)]
    row_index = lax.axis_index("row")
    me = jnp.reshape(row_index, (1,)).astype(jnp.int32)

    def to_x(a):
        return lax.ppermute(a, "row", across_x)

    def to_y(a):
        return lax.ppermute(a, "row", across_y)

    def other(a):
        return lax.ppermute(a, "rep", swap)

    def along(a, shift):
        return lax.ppermute(a, "col", [(i, (i + shift) % n_col) for i in range(n_col)])

    def f32(a):
        return a.astype(jnp.float32)

    peer = 1 - jnp.reshape(lax.axis_index("rep"), (1,)).astype(jnp.int32)

    def quarters(*ks):
        return jnp.concatenate([me ^ k for k in ks] + [peer])

    own_x, own_c = patches[0], cotangent[0]
    moment_in, moment_out = moment_in[0], moment_out[0]

    xs = [own_x] + [along(own_x, b) for b in range(1, n_col)]
    cs = [own_c] + [along(own_c, b) for b in range(1, n_col)]
    every_moment_out = lax.all_gather(moment_out, "rep")
    every_moment_in = lax.all_gather(moment_in, "rep")

    send_a, pre_a, send_b, pre_b, x_all = project(me, xs, w_in, False, n_row)
    pre_got_a, pre_got_b = to_x(send_a), to_y(send_b)
    send_a, back_a, send_b, back_b, c_all = project(me, cs, w_out, True, n_row, after=(x_all,))
    back_got_a, back_got_b = to_x(send_a), to_y(send_b)
    scale = (1.0 - momentum_decay) / (vote_scale * math.sqrt(x_all.shape[0]))

    late_a, late_b = late_sums(pre_a, pre_got_a, pre_b, pre_got_b, after=(c_all,))
    pre_late_a, pre_late_b = to_y(late_a), to_x(late_b)
    late_a, late_b = late_sums(back_a, back_got_a, back_b, back_got_b, after=(late_a,))
    back_late_a, back_late_b = to_y(late_a), to_x(late_b)

    bf16 = jnp.bfloat16
    hidden, pack, steep = finish(
        hidden_body, "hidden", ((2, bf16), (4, bf16), (2, jnp.float32)),
        (pre_a, pre_got_a, pre_late_a, pre_b, pre_got_b, pre_late_b), c_all, after=(late_a,),
    )
    hidden_x, hidden_y, hidden_other = to_x(hidden), to_y(hidden), other(pack)
    slope, pack = finish(
        slope_body, "slope", ((2, bf16), (4, bf16)),
        (back_a, back_got_a, back_late_a, back_b, back_got_b, back_late_b), x_all, (steep,),
    )
    slope_x, slope_y, slope_other = to_x(slope), to_y(slope), other(pack)

    both_c, both_out = (c_all, hidden_other), (moment_out, every_moment_out)
    both_x, both_in = (x_all, slope_other), (moment_in, every_moment_in)

    tally_out = tally(
        "out", quarters(0), both_c, (hidden, hidden_other), both_out, None, scale, after=(slope,)
    )
    near_a, near_b = forward(hidden_x, hidden_y, after=(tally_out,))
    hidden_far_a, hidden_far_b = to_y(near_a), to_x(near_b)
    far_a, far_b = forward(slope_x, slope_y, after=(near_a,))
    tally_in = tally(
        "in", quarters(0), both_x, (slope, slope_other), both_in, None, scale, after=(far_a,)
    )
    slope_far_a, slope_far_b = to_y(far_a), to_x(far_b)
    column = jnp.reshape(lax.axis_index("col"), (1,)).astype(jnp.int32)
    parts, hidden_rest = mix(
        jnp.concatenate([me, column]),
        [(a, h) for a in (hidden, hidden_x, hidden_y) for h in range(2)]
        + [(hidden_far_a, 0), (hidden_far_b, 0)],
        w_out,
        n_col,
        after=(tally_in, slope_far_a, slope_far_b),
    )
    mixed = lax.psum_scatter(parts, "col", scatter_dimension=0, tiled=True).astype(bf16)
    hidden_rest_other = other(hidden_rest)
    near = jnp.concatenate([slope_x, slope_y])
    near_other = other(near)
    tally_out = tally(
        "out", quarters(1, 2, 3), both_c, (hidden_rest, hidden_rest_other), both_out, tally_out,
        scale, after=(near, far_a),
    )
    tally_in = tally(
        "in", quarters(1, 2), both_x, (near, near_other), both_in, tally_in, scale,
        after=(tally_out,),
    )
    far = jnp.stack([slope_far_a, slope_far_b])
    tally_in = tally("in", quarters(3), both_x, (far, other(far)), both_in, tally_in, scale)
    return mixed, tally_in, tally_out


def solution(mesh):
    in_specs = (
        P("rep", "col", "row"),
        P("rep", "col", "row"),
        P("row", "col"),
        P("col", "row"),
        P("rep", "row", "col"),
        P("rep", "col", "row"),
    )
    out_specs = (P("rep", "col", "row"), P("row", "col"), P("col", "row"))
    sizes = dict(mesh.shape)
    if sizes["row"] == 4 and sizes["rep"] == 2:
        body = functools.partial(shards_square, sizes["col"], sizes["rep"])
    else:
        body = shards_plain
    return jax.shard_map(body, mesh=mesh, in_specs=in_specs, out_specs=out_specs, check_vma=False)
```

time: 451 us -> 264 us (0.59)
  waiting for transfers between devices: 256 us -> 81.9 us
  Pallas kernels: 0 us -> 131 us
  matrix products: 74.7 us -> 0 us
  local copies, waits for them, and re-layouts: 65.7 us -> 6.33 us
  blocking collectives: 32.7 us -> 0 us
  starting transfers between devices: 0.42 us -> 25.7 us
    pallas_call x0 -> x14, Pallas kernels: none -> 131 us  [the longest x5 75.2 us: tally(): pl.pallas_call(body, grid_spec=pltpu.PrefetchScalarGridSpec(num_scalar_pr...]
    psum x1 -> x0, waiting for transfers between devices: 116 us -> none  [shards(): lax.psum(vote_first, 'rep').astype(jnp.float32)]
    reduce_scatter x3 -> x1, waiting for transfers between devices: 106 us -> 0.01 us  [shards_square(): lax.psum_scatter(parts, 'col', scatter_dimension=0, tiled=True).astype(bf16)]
    ppermute x0 -> x27, waiting for transfers between devices: none -> 80.5 us  [the longest x8 37.7 us: to_x(): return lax.ppermute(a, 'row', across_x)]
    dot_general x5 -> x0, matrix products: 74.7 us -> none  [the longest x1 20 us: shards(): lax.dot_general(inputs, slope, (((0,), (0,)), ((), ())), preferred_elemen...]
    unnamed x5 -> x19, local copies, waits for them, and re-layouts: 65.7 us -> 5.02 us
    all_gather x2, waiting for transfers between devices: 33.7 us -> 0.01 us  [the longest x1 0.01 us: shards_square(): every_moment_out = lax.all_gather(moment_out, 'rep')]
    all_gather x2 -> x0, blocking collectives: 32.7 us -> none  [the longest x1 16.7 us: shards(): grads = lax.all_gather(cotangent[0], 'col', axis=0, tiled=True)]
  transfers between devices with their start and end apart: 6 -> 30, of which waited for: 6 -> 13; matrix products, arithmetic and copies ran while one was open for 20% -> 2% of each run, Pallas kernels for 0% -> 45%
where the time goes in v1:
time: 264 us; the launch traced here: 262 us
  Pallas kernels  131 us (50%)
  waiting for transfers between devices  81.9 us (31%)
  starting transfers between devices  25.7 us (10%)
  between operations  13.8 us (5%)
  local copies, waits for them, and re-layouts  6.33 us (2%)
  other arithmetic  3.26 us (1%)
    pallas_call x5, Pallas kernels, tally(): pl.pallas_call(body, grid_spec=pltpu.PrefetchScalarGridSpec(num_scalar_pr...  75.2 us
    ppermute x8, waiting for transfers between devices, to_x(): return lax.ppermute(a, 'row', across_x)  37.7 us
    pallas_call x2, Pallas kernels, project(): pl.pallas_call(functools.partial(project_body, transposed, len(toks)), gr...  28.5 us
    ppermute x8, waiting for transfers between devices, to_y(): return lax.ppermute(a, 'row', across_y)  22.2 us
    ppermute x6, waiting for transfers between devices, along(): lax.ppermute(a, 'col', [(i, (i + shift) % n_col) for i in range(n_col)])  20.7 us
    pallas_call x1, Pallas kernels, mix(): pl.pallas_call(functools.partial(mix_body, n_half, n_col, len(after)), gr...  14.1 us
    ppermute x6, starting transfers between devices, along(): lax.ppermute(a, 'col', [(i, (i + shift) % n_col) for i in range(n_col)])  8.15 us
    pallas_call x2, Pallas kernels, finish(): pl.pallas_call(body, grid=(1,), in_specs=[kept, kept, late] * 2 + [pl.Blo...  7.46 us
  transfers between devices with their start and end apart: 30, of which 13 were waited for; matrix products, arithmetic and copies ran while one was open for 2% of the time, Pallas kernels for 45%

profile of v1, /device:TPU:9, one launch (start us, length us, event | category | flops | bytes accessed | tf_op | source)
XLA Modules:
  0.0 261.8 jit_solution(12146721669417446475)
XLA Ops:
  8.8 1.3 collective-permute-start
  10.1 1.0 collective-permute-start.1
  11.2 1.4 collective-permute-start.2
  12.6 3.2 %collective-permute-start.6 = (bf16[64,1536]{1,0:T(8,128)(2,1)S(1)}, bf16[64,1536]{1,0:T(8,128)(2,1)S(1)}, u32[]{:S(2)}, u32[]{:S(2)}) collective-permute-start(bf16[64,1536]{1,0:T(8,128)(2,1)S(1)} %bitcast.14), channel_id=1, source_target_pairs={{0,4},{2,6},{4,0},{6,2},{1,5},{3,7},{5,1},{7,3},{8,12},{10,14},{12... | collective-permute-start | bytes 589832 | tf_op jit(solution)/shard_map/ppermute | solution.py:377
  15.8 1.2 collective-permute-start.7
  17.0 9.4 %collective-permute-done.1.refs_2_ = bf16[64,1536]{1,0:T(8,128)(2,1)S(1)} collective-permute-done((bf16[64,1536]{1,0:T(8,128)(2,1)S(1)}, bf16[64,1536]{1,0:T(8,128)(2,1)S(1)}, u32[]{:S(2)}, u32[]{:S(2)}) %collective-permute-start.1) | collective-permute-done | bytes 196640 | tf_op jit(solution)/shard_map/ppermute | solution.py:377
  26.4 11.3 %collective-permute-done.2.refs_3_ = bf16[64,1536]{1,0:T(8,128)(2,1)S(1)} collective-permute-done((bf16[64,1536]{1,0:T(8,128)(2,1)S(1)}, bf16[64,1536]{1,0:T(8,128)(2,1)S(1)}, u32[]{:S(2)}, u32[]{:S(2)}) %collective-permute-start.2) | collective-permute-done | bytes 196640 | tf_op jit(solution)/shard_map/ppermute | solution.py:377
  37.6 15.7 %project_pre.1 = (bf16[2,256,768]{2,1,0:T(8,128)(2,1)S(1)}, f32[2,256,768]{2,1,0:T(8,128)S(1)}, bf16[2,256,768]{2,1,0:T(8,128)(2,1)S(1)}, f32[2,256,768]{2,1,0:T(8,128)}, bf16[256,1536]{1,0:T(8,128)(2,1)S(1)}) custom-call(s32[1]{0:T(128)} %bitcast.idx, bf16[64,1536]{1,0:T(8,128)(2,1)S(1)} %bitcast.12, bf16[64,1536]{1,0:T(8,128)(2,1)S(1)} %collective-permute-done.refs_1_, ...), custom_call_target="tpu_custom_call" | custom-call | flops 4831838208 | bytes 24379392 | tf_op jit(solution)/shard_map/project_pre/pallas_call | solution.py:118
  53.4 1.2 collective-permute-start.3
  54.5 1.3 collective-permute-start.4
  55.8 12.8 %project_back.1 = (bf16[2,256,768]{2,1,0:T(8,128)(2,1)S(1)}, f32[2,256,768]{2,1,0:T(8,128)S(1)}, bf16[2,256,768]{2,1,0:T(8,128)(2,1)S(1)}, f32[2,256,768]{2,1,0:T(8,128)}, bf16[256,1536]{1,0:T(8,128)(2,1)S(1)}) custom-call(s32[1]{0:T(128)} %bitcast.idx, bf16[64,1536]{1,0:T(8,128)(2,1)S(1)} %bitcast.16, bf16[64,1536]{1,0:T(8,128)(2,1)S(1)} %collective-permute-done.5.refs_1_, ...), custom_call_target="tpu_custom_call" | custom-call | flops 4831838208 | bytes 24379392 | tf_op jit(solution)/shard_map/project_back/pallas_call | solution.py:118
  69.1 2.8 %collective-permute-done.3.got_a.refs_1_ = bf16[2,256,768]{2,1,0:T(8,128)(2,1)S(1)} collective-permute-done((bf16[2,256,768]{2,1,0:T(8,128)(2,1)S(1)}, bf16[2,256,768]{2,1,0:T(8,128)(2,1)S(1)}, u32[]{:S(2)}, u32[]{:S(2)}) %collective-permute-start.3) | collective-permute-done | bytes 786464 | tf_op jit(solution)/shard_map/ppermute | solution.py:368
  71.9 0.9 collective-permute-done.4.got_b.refs_4_
  72.8 1.4 late_sums.2
  74.2 1.3 collective-permute-start.8
  75.8 13.0 %collective-permute-done.10.got_a.refs_1_ = bf16[2,256,768]{2,1,0:T(8,128)(2,1)S(1)} collective-permute-done((bf16[2,256,768]{2,1,0:T(8,128)(2,1)S(1)}, bf16[2,256,768]{2,1,0:T(8,128)(2,1)S(1)}, u32[]{:S(2)}, u32[]{:S(2)}) %collective-permute-start.10) | collective-permute-done | bytes 786464 | tf_op jit(solution)/shard_map/ppermute | solution.py:368
  88.8 0.9 collective-permute-done.11.got_b.refs_4_
  89.8 8.3 %collective-permute-done.8.refs_2_ = bf16[256,768]{1,0:T(8,128)(2,1)S(1)} collective-permute-done((bf16[256,768]{1,0:T(8,128)(2,1)S(1)}, bf16[256,768]{1,0:T(8,128)(2,1)S(1)}, u32[]{:S(2)}, u32[]{:S(2)}) %collective-permute-start.8) | collective-permute-done | bytes 393248 | tf_op jit(solution)/shard_map/ppermute | solution.py:371
  98.1 3.8 %hidden.1 = (bf16[2,256,768]{2,1,0:T(8,128)(2,1)}, bf16[4,256,768]{2,1,0:T(8,128)(2,1)S(1)}, f32[2,256,768]{2,1,0:T(8,128)}) custom-call(f32[2,256,768]{2,1,0:T(8,128)} %copy-done.3, bf16[2,256,768]{2,1,0:T(8,128)(2,1)S(1)} %collective-permute-done.3.got_a.refs_1_, bf16[256,768]{1,0:T(8,128)(2,1)S(1)} %collective-permute-done.8.refs_2_, ...), custom_call_target="tpu_custom_call" | custom-call | tf_op jit(solution)/shard_map/hidden/pallas_call | solution.py:236
  101.9 1.8 collective-permute-start.14
  103.7 1.2 collective-permute-start.15
  105.2 9.2 %collective-permute-done.15.refs_2_ = bf16[256,768]{1,0:T(8,128)(2,1)S(1)} collective-permute-done((bf16[256,768]{1,0:T(8,128)(2,1)S(1)}, bf16[256,768]{1,0:T(8,128)(2,1)S(1)}, u32[]{:S(2)}, u32[]{:S(2)}) %collective-permute-start.15) | collective-permute-done | bytes 393248 | tf_op jit(solution)/shard_map/ppermute | solution.py:371
  114.4 0.9 collective-permute-done.16.refs_5_
  115.3 3.6 %slope.1 = (bf16[2,256,768]{2,1,0:T(8,128)(2,1)}, bf16[4,256,768]{2,1,0:T(8,128)(2,1)}) custom-call(f32[2,256,768]{2,1,0:T(8,128)} %copy-done.4, bf16[2,256,768]{2,1,0:T(8,128)(2,1)S(1)} %collective-permute-done.10.got_a.refs_1_, bf16[256,768]{1,0:T(8,128)(2,1)S(1)} %collective-permute-done.15.refs_2_, f32[2,256,768]{2,1,0:T(8,128)} %get-tuple-element.38.keep_b.refs_3_, ...), custom_call_target="tpu_custom_call" | custom-call | tf_op jit(solution)/shard_map/slope/pallas_call | solution.py:236
  119.0 1.1 collective-permute-start.19
  120.6 1.2 collective-permute-start.20
  121.8 1.1 copy-done
  122.9 1.2 collective-permute-start.21
  124.2 1.4 copy-done.1
  125.6 10.1 %tally_out.2.refs_0_.rest_0_ = bf16[6144,1536]{1,0:T(8,128)(2,1)} custom-call(s32[2]{0:T(128)S(1)} %pad_add_fusion.4.idx, bf16[256,1536]{1,0:T(8,128)(2,1)S(1)} %get-tuple-element.33.refs_0_.refs_6_.c0, bf16[4,256,768]{2,1,0:T(8,128)(2,1)S(1)} %copy-done.1, bf16[2,256,768]{2,1,0:T(8,128)(2,1)} %get-tuple-element.41.s0.refs_0_.refs_1_, ...), custom_call_target="tpu_custom_call" | custom-call | flops 2415919104 | bytes 14155776 | tf_op jit(solution)/shard_map/tally_out/pallas_call | solution.py:341
  135.7 3.9 %collective-permute-done.12.from_x.refs_2_.refs_3_ = bf16[2,256,768]{2,1,0:T(8,128)(2,1)} collective-permute-done((bf16[2,256,768]{2,1,0:T(8,128)(2,1)}, bf16[2,256,768]{2,1,0:T(8,128)(2,1)}, u32[]{:S(2)}, u32[]{:S(2)}) %collective-permute-start.12) | collective-permute-done | bytes 786464 | tf_op jit(solution)/shard_map/ppermute | solution.py:368
  139.5 2.1 forward.2
  141.9 14.5 %collective-permute-done.20.from_x = bf16[2,256,768]{2,1,0:T(8,128)(2,1)} collective-permute-done((bf16[2,256,768]{2,1,0:T(8,128)(2,1)}, bf16[2,256,768]{2,1,0:T(8,128)(2,1)}, u32[]{:S(2)}, u32[]{:S(2)}) %collective-permute-start.20) | collective-permute-done | bytes 786464 | tf_op jit(solution)/shard_map/ppermute | solution.py:368
  156.4 1.9 forward.3
  158.5 1.1 collective-permute-start.23
  160.1 10.2 %tally_in.3.refs_9_.rest_0_ = bf16[1536,6144]{1,0:T(8,128)(2,1)} custom-call(s32[2]{0:T(128)S(1)} %pad_add_fusion.4.idx, bf16[256,1536]{1,0:T(8,128)(2,1)S(1)} %get-tuple-element.32.refs_5_.refs_6_.x0, bf16[4,256,768]{2,1,0:T(8,128)(2,1)S(1)} %collective-permute-done.19.x1.s1, bf16[2,256,768]{2,1,0:T(8,128)(2,1)} %get-tuple-element.45.rest_0_.s0, ...), custom_call_target="tpu_custom_call" | custom-call | flops 2415919104 | bytes 14155776 | tf_op jit(solution)/shard_map/tally_in/pallas_call | solution.py:341
  170.3 2.9 %collective-permute-done.22.refs_10_ = bf16[256,768]{1,0:T(8,128)(2,1)} collective-permute-done((bf16[256,768]{1,0:T(8,128)(2,1)S(1)}, bf16[256,768]{1,0:T(8,128)(2,1)}, u32[]{:S(2)}, u32[]{:S(2)}) %collective-permute-start.22) | collective-permute-done | bytes 393248 | tf_op jit(solution)/shard_map/ppermute | solution.py:371
  173.2 2.6 collective-permute-done.18.refs_7_
  175.8 14.1 %mix.1 = (f32[4,64,1536]{2,1,0:T(8,128)S(1)}, bf16[6,256,768]{2,1,0:T(8,128)(2,1)}) custom-call(s32[2]{0:T(128)S(1)} %pad_add_fusion.idx, bf16[2,256,768]{2,1,0:T(8,128)(2,1)} %get-tuple-element.41.s0.refs_0_.refs_1_, bf16[2,256,768]{2,1,0:T(8,128)(2,1)} %get-tuple-element.41.s0.refs_0_.refs_1_, ...), custom_call_target="tpu_custom_call" | custom-call | flops 4831838208 | bytes 26738688 | tf_op jit(solution)/shard_map/mix/pallas_call | solution.py:166
  189.9 1.2 copy-done.6
  191.1 3.0 %collective-permute-start.26 = (bf16[6,256,768]{2,1,0:T(8,128)(2,1)}, bf16[6,256,768]{2,1,0:T(8,128)(2,1)}, u32[]{:S(2)}, u32[]{:S(2)}) collective-permute-start(bf16[6,256,768]{2,1,0:T(8,128)(2,1)} %get-tuple-element.52.s0), channel_id=1, source_target_pairs={{0,1},{1,0},{2,3},{3,2},{4,5},{5,4},{6,7},{7,6},{8,9},{9,8},{10,11... | collective-permute-start | bytes 7077896 | tf_op jit(solution)/shard_map/ppermute | solution.py:374
  194.1 1.2 constant_dynamic-update-slice_fusion.1
  195.3 1.3 constant_dynamic-update-slice_fusion.rest_1_.s0
  196.9 1.2 pad_maximum_fusion.s0
  198.7 26.9 %tally_out.3.rest_1_ = bf16[6144,1536]{1,0:T(8,128)(2,1)} custom-call(s32[4]{0:T(128)S(1)} %pad_add_fusion.3.idx, bf16[256,1536]{1,0:T(8,128)(2,1)S(1)} %get-tuple-element.33.refs_0_.refs_6_.c0, bf16[4,256,768]{2,1,0:T(8,128)(2,1)S(1)} %copy-done.2, bf16[6,256,768]{2,1,0:T(8,128)(2,1)} %get-tuple-element.52.s0, ...), custom_call_target="tpu_custom_call", output_to_operand_aliasing={{}: (7, {})} | custom-call | flops 7247757312 | bytes 42467328 | tf_op jit(solution)/shard_map/tally_out/pallas_call | solution.py:341
  225.6 17.8 %tally_in.4.rest_0_ = bf16[1536,6144]{1,0:T(8,128)(2,1)} custom-call(s32[3]{0:T(128)S(1)} %pad_add_fusion.2.idx, bf16[256,1536]{1,0:T(8,128)(2,1)S(1)} %get-tuple-element.32.refs_5_.refs_6_.x0, bf16[4,256,768]{2,1,0:T(8,128)(2,1)S(1)} %collective-permute-done.19.x1.s1, ...), custom_call_target="tpu_custom_call", output_to_operand_aliasing={{}: (7, {})} | custom-call | flops 4831838208 | bytes 28311552 | tf_op jit(solution)/shard_map/tally_in/pallas_call | solution.py:341
  243.4 10.2 %tally_in.5 = bf16[1536,6144]{1,0:T(8,128)(2,1)} custom-call(s32[2]{0:T(128)S(1)} %pad_add_fusion.1.idx, bf16[256,1536]{1,0:T(8,128)(2,1)S(1)} %get-tuple-element.32.refs_5_.refs_6_.x0, bf16[4,256,768]{2,1,0:T(8,128)(2,1)S(1)} %collective-permute-done.19.x1.s1, bf16[2,256,768]{2,1,0:T(8,128)(2,1)S(1)} %pad_maximum_fusion.s0, ...), custom_call_target="tpu_custom_call", output_to_operand_aliasing={{}: (7, {})} | custom-call | flops 2415919104 | bytes 14155776 | tf_op jit(solution)/shard_map/tally_in/pallas_call | solution.py:341
  253.6 1.7 convert_element_type.3
  (56 shorter events, 5.3 us)
Async XLA Ops:
  7.2 117.0 %all-gather.3.cloned.1.call-start = ((), (), s32[]{:S(2)}) async-start(), calls=%async_computation.1 | async-start | bytes 56623104 | tf_op jit(solution)/shard_map/all_gather | solution.py:392
  7.9 0.9 copy-start.7
  7.9 4.7 %copy-start.8 = (bf16[1,64,1536]{2,1,0:T(8,128)(2,1)S(1)}, bf16[1,64,1536]{2,1,0:T(8,128)(2,1)}, u32[]{:S(2)}) copy-start(bf16[1,64,1536]{2,1,0:T(8,128)(2,1)} %param.7) | copy-start | bytes 589828
  7.9 152.2 %all-gather.5.cloned.1.call-start = ((), (), s32[]{:S(2)}) async-start(), calls=%async_computation.2 | async-start | bytes 56623104 | tf_op jit(solution)/shard_map/all_gather | solution.py:393
  8.7 244.9 %reduce-scatter.2.cloned.1.call-start = ((), (), s32[]{:S(2)}) async-start(), calls=%async_computation.3 | async-start | bytes 1966080 | tf_op jit(solution)/shard_map/reduce_scatter | solution.py:440
  8.8 7.0 %collective-permute-start = (bf16[64,1536]{1,0:T(8,128)(2,1)S(1)}, bf16[64,1536]{1,0:T(8,128)(2,1)S(1)}, u32[]{:S(2)}, u32[]{:S(2)}) collective-permute-start(bf16[64,1536]{1,0:T(8,128)(2,1)S(1)} %bitcast.9), channel_id=1, source_target_pairs={{0,2},{2,4},{4,6},{6,0},{1,3},{3,5},{5,7},{7,1},{8,10},{10,12},{12... | collective-permute-start | bytes 589832 | tf_op jit(solution)/shard_map/ppermute | solution.py:377
  10.1 16.3 %collective-permute-start.1 = (bf16[64,1536]{1,0:T(8,128)(2,1)S(1)}, bf16[64,1536]{1,0:T(8,128)(2,1)S(1)}, u32[]{:S(2)}, u32[]{:S(2)}) collective-permute-start(bf16[64,1536]{1,0:T(8,128)(2,1)S(1)} %bitcast.10), channel_id=1, source_target_pairs={{0,4},{2,6},{4,0},{6,2},{1,5},{3,7},{5,1},{7,3},{8,12},{10,14},{12... | collective-permute-start | bytes 589832 | tf_op jit(solution)/shard_map/ppermute | solution.py:377
  11.2 26.5 %collective-permute-start.2 = (bf16[64,1536]{1,0:T(8,128)(2,1)S(1)}, bf16[64,1536]{1,0:T(8,128)(2,1)S(1)}, u32[]{:S(2)}, u32[]{:S(2)}) collective-permute-start(bf16[64,1536]{1,0:T(8,128)(2,1)S(1)} %bitcast.11), channel_id=1, source_target_pairs={{0,6},{2,0},{4,2},{6,4},{1,7},{3,1},{5,3},{7,5},{8,14},{10,8},{12,... | collective-permute-start | bytes 589832 | tf_op jit(solution)/shard_map/ppermute | solution.py:377
  12.6 43.2 %collective-permute-start.5 = (bf16[64,1536]{1,0:T(8,128)(2,1)S(1)}, bf16[64,1536]{1,0:T(8,128)(2,1)S(1)}, u32[]{:S(2)}, u32[]{:S(2)}) collective-permute-start(bf16[64,1536]{1,0:T(8,128)(2,1)S(1)} %bitcast.13), channel_id=1, source_target_pairs={{0,2},{2,4},{4,6},{6,0},{1,3},{3,5},{5,7},{7,1},{8,10},{10,12},{12... | collective-permute-start | bytes 589832 | tf_op jit(solution)/shard_map/ppermute | solution.py:377
  12.6 43.2 %collective-permute-start.6 = (bf16[64,1536]{1,0:T(8,128)(2,1)S(1)}, bf16[64,1536]{1,0:T(8,128)(2,1)S(1)}, u32[]{:S(2)}, u32[]{:S(2)}) collective-permute-start(bf16[64,1536]{1,0:T(8,128)(2,1)S(1)} %bitcast.14), channel_id=1, source_target_pairs={{0,4},{2,6},{4,0},{6,2},{1,5},{3,7},{5,1},{7,3},{8,12},{10,14},{12... | collective-permute-start | bytes 589832 | tf_op jit(solution)/shard_map/ppermute | solution.py:377
  15.8 40.0 %collective-permute-start.7 = (bf16[64,1536]{1,0:T(8,128)(2,1)S(1)}, bf16[64,1536]{1,0:T(8,128)(2,1)S(1)}, u32[]{:S(2)}, u32[]{:S(2)}) collective-permute-start(bf16[64,1536]{1,0:T(8,128)(2,1)S(1)} %bitcast.15), channel_id=1, source_target_pairs={{0,6},{2,0},{4,2},{6,4},{1,7},{3,1},{5,3},{7,5},{8,14},{10,8},{12,... | collective-permute-start | bytes 589832 | tf_op jit(solution)/shard_map/ppermute | solution.py:377
  53.4 19.4 %copy-start.3 = (f32[2,256,768]{2,1,0:T(8,128)}, f32[2,256,768]{2,1,0:T(8,128)S(1)}, u32[]{:S(2)}) copy-start(f32[2,256,768]{2,1,0:T(8,128)S(1)} %get-tuple-element.28.keep_a.refs_0_) | copy-start | bytes 4718596
  53.4 18.6 %collective-permute-start.3 = (bf16[2,256,768]{2,1,0:T(8,128)(2,1)S(1)}, bf16[2,256,768]{2,1,0:T(8,128)(2,1)S(1)}, u32[]{:S(2)}, u32[]{:S(2)}) collective-permute-start(bf16[2,256,768]{2,1,0:T(8,128)(2,1)S(1)} %get-tuple-element.29), channel_id=1, source_target_pairs={{0,8},{8,0},{16,24},{24,16},{1,9},{9,1},{17,25},{25,17},{2,10},{10... | collective-permute-start | bytes 2359304 | tf_op jit(solution)/shard_map/ppermute | solution.py:368
  54.5 18.2 %collective-permute-start.4 = (bf16[2,256,768]{2,1,0:T(8,128)(2,1)S(1)}, bf16[2,256,768]{2,1,0:T(8,128)(2,1)S(1)}, u32[]{:S(2)}, u32[]{:S(2)}) collective-permute-start(bf16[2,256,768]{2,1,0:T(8,128)(2,1)S(1)} %get-tuple-element.31), channel_id=1, source_target_pairs={{0,16},{8,24},{16,0},{24,8},{1,17},{9,25},{17,1},{25,9},{2,18},{10... | collective-permute-start | bytes 2359304 | tf_op jit(solution)/shard_map/ppermute | solution.py:371
  68.6 21.0 %copy-start.4 = (f32[2,256,768]{2,1,0:T(8,128)}, f32[2,256,768]{2,1,0:T(8,128)S(1)}, u32[]{:S(2)}) copy-start(f32[2,256,768]{2,1,0:T(8,128)S(1)} %get-tuple-element.36.keep_a.refs_0_) | copy-start | bytes 4718596
  68.6 20.2 %collective-permute-start.10 = (bf16[2,256,768]{2,1,0:T(8,128)(2,1)S(1)}, bf16[2,256,768]{2,1,0:T(8,128)(2,1)S(1)}, u32[]{:S(2)}, u32[]{:S(2)}) collective-permute-start(bf16[2,256,768]{2,1,0:T(8,128)(2,1)S(1)} %get-tuple-element.37), channel_id=1, source_target_pairs={{0,8},{8,0},{16,24},{24,16},{1,9},{9,1},{17,25},{25,17},{2,10},{10... | collective-permute-start | bytes 2359304 | tf_op jit(solution)/shard_map/ppermute | solution.py:368
  68.8 20.8 %collective-permute-start.11 = (bf16[2,256,768]{2,1,0:T(8,128)(2,1)S(1)}, bf16[2,256,768]{2,1,0:T(8,128)(2,1)S(1)}, u32[]{:S(2)}, u32[]{:S(2)}) collective-permute-start(bf16[2,256,768]{2,1,0:T(8,128)(2,1)S(1)} %get-tuple-element.39), channel_id=1, source_target_pairs={{0,16},{8,24},{16,0},{24,8},{1,17},{9,25},{17,1},{25,9},{2,18},{10... | collective-permute-start | bytes 2359304 | tf_op jit(solution)/shard_map/ppermute | solution.py:371
  72.8 16.9 %copy-start.5 = (f32[2,256,768]{2,1,0:T(8,128)S(1)}, f32[2,256,768]{2,1,0:T(8,128)}, u32[]{:S(2)}) copy-start(f32[2,256,768]{2,1,0:T(8,128)} %get-tuple-element.38.keep_b.refs_3_) | copy-start | bytes 4718596
  74.2 23.9 %collective-permute-start.8 = (bf16[256,768]{1,0:T(8,128)(2,1)S(1)}, bf16[256,768]{1,0:T(8,128)(2,1)S(1)}, u32[]{:S(2)}, u32[]{:S(2)}) collective-permute-start(bf16[256,768]{1,0:T(8,128)(2,1)S(1)} %get-tuple-element.34.refs_0_), channel_id=1, source_target_pairs={{0,16},{8,24},{16,0},{24,8},{1,17},{9,25},{17,1},{25,9},{2,18},{10... | collective-permute-start | bytes 1179656 | tf_op jit(solution)/shard_map/ppermute | solution.py:371
  75.5 22.6 %collective-permute-start.9 = (bf16[256,768]{1,0:T(8,128)(2,1)S(1)}, bf16[256,768]{1,0:T(8,128)(2,1)S(1)}, u32[]{:S(2)}, u32[]{:S(2)}) collective-permute-start(bf16[256,768]{1,0:T(8,128)(2,1)S(1)} %get-tuple-element.35), channel_id=1, source_target_pairs={{0,8},{8,0},{16,24},{24,16},{1,9},{9,1},{17,25},{25,17},{2,10},{10... | collective-permute-start | bytes 1179656 | tf_op jit(solution)/shard_map/ppermute | solution.py:368
  101.9 19.9 %collective-permute-start.14 = (bf16[4,256,768]{2,1,0:T(8,128)(2,1)S(1)}, bf16[4,256,768]{2,1,0:T(8,128)(2,1)S(1)}, u32[]{:S(2)}, u32[]{:S(2)}) collective-permute-start(bf16[4,256,768]{2,1,0:T(8,128)(2,1)S(1)} %get-tuple-element.42), channel_id=1, source_target_pairs={{0,1},{1,0},{2,3},{3,2},{4,5},{5,4},{6,7},{7,6},{8,9},{9,8},{10,11... | collective-permute-start | bytes 4718600 | tf_op jit(solution)/shard_map/ppermute | solution.py:374
  103.7 10.7 %collective-permute-start.15 = (bf16[256,768]{1,0:T(8,128)(2,1)S(1)}, bf16[256,768]{1,0:T(8,128)(2,1)S(1)}, u32[]{:S(2)}, u32[]{:S(2)}) collective-permute-start(bf16[256,768]{1,0:T(8,128)(2,1)S(1)} %get-tuple-element.40.refs_7_), channel_id=1, source_target_pairs={{0,16},{8,24},{16,0},{24,8},{1,17},{9,25},{17,1},{25,9},{2,18},{10... | collective-permute-start | bytes 1179656 | tf_op jit(solution)/shard_map/ppermute | solution.py:371
  104.9 10.4 %collective-permute-start.16 = (bf16[256,768]{1,0:T(8,128)(2,1)S(1)}, bf16[256,768]{1,0:T(8,128)(2,1)S(1)}, u32[]{:S(2)}, u32[]{:S(2)}) collective-permute-start(bf16[256,768]{1,0:T(8,128)(2,1)S(1)} %get-tuple-element.43), channel_id=1, source_target_pairs={{0,8},{8,0},{16,24},{24,16},{1,9},{9,1},{17,25},{25,17},{2,10},{10... | collective-permute-start | bytes 1179656 | tf_op jit(solution)/shard_map/ppermute | solution.py:368
  119.0 41.1 %collective-permute-start.19 = (bf16[4,256,768]{2,1,0:T(8,128)(2,1)}, bf16[4,256,768]{2,1,0:T(8,128)(2,1)S(1)}, u32[]{:S(2)}, u32[]{:S(2)}) collective-permute-start(bf16[4,256,768]{2,1,0:T(8,128)(2,1)} %get-tuple-element.48), channel_id=1, source_target_pairs={{0,1},{1,0},{2,3},{3,2},{4,5},{5,4},{6,7},{7,6},{8,9},{9,8},{10,11... | collective-permute-start | bytes 4718600 | tf_op jit(solution)/shard_map/ppermute | solution.py:374
  120.1 19.5 %collective-permute-start.12 = (bf16[2,256,768]{2,1,0:T(8,128)(2,1)}, bf16[2,256,768]{2,1,0:T(8,128)(2,1)}, u32[]{:S(2)}, u32[]{:S(2)}) collective-permute-start(bf16[2,256,768]{2,1,0:T(8,128)(2,1)} %get-tuple-element.41.s0.refs_0_.refs_1_), channel_id=1, source_target_pairs={{0,8},{8,0},{16,24},{24,16},{1,9},{9,1},{17,25},{25,17},{2,10},{10... | collective-permute-start | bytes 2359304 | tf_op jit(solution)/shard_map/ppermute | solution.py:368
  120.4 19.2 %collective-permute-start.13 = (bf16[2,256,768]{2,1,0:T(8,128)(2,1)}, bf16[2,256,768]{2,1,0:T(8,128)(2,1)}, u32[]{:S(2)}, u32[]{:S(2)}) collective-permute-start(bf16[2,256,768]{2,1,0:T(8,128)(2,1)} %get-tuple-element.41.s0.refs_0_.refs_1_), channel_id=1, source_target_pairs={{0,16},{8,24},{16,0},{24,8},{1,17},{9,25},{17,1},{25,9},{2,18},{10... | collective-permute-start | bytes 2359304 | tf_op jit(solution)/shard_map/ppermute | solution.py:371
  120.6 35.8 %collective-permute-start.20 = (bf16[2,256,768]{2,1,0:T(8,128)(2,1)}, bf16[2,256,768]{2,1,0:T(8,128)(2,1)}, u32[]{:S(2)}, u32[]{:S(2)}) collective-permute-start(bf16[2,256,768]{2,1,0:T(8,128)(2,1)} %get-tuple-element.45.rest_0_.s0), channel_id=1, source_target_pairs={{0,8},{8,0},{16,24},{24,16},{1,9},{9,1},{17,25},{25,17},{2,10},{10... | collective-permute-start | bytes 2359304 | tf_op jit(solution)/shard_map/ppermute | solution.py:368
  121.8 1.1 copy-start
  122.9 33.5 %collective-permute-start.21 = (bf16[2,256,768]{2,1,0:T(8,128)(2,1)}, bf16[2,256,768]{2,1,0:T(8,128)(2,1)}, u32[]{:S(2)}, u32[]{:S(2)}) collective-permute-start(bf16[2,256,768]{2,1,0:T(8,128)(2,1)} %get-tuple-element.45.rest_0_.s0), channel_id=1, source_target_pairs={{0,16},{8,24},{16,0},{24,8},{1,17},{9,25},{17,1},{25,9},{2,18},{10... | collective-permute-start | bytes 2359304 | tf_op jit(solution)/shard_map/ppermute | solution.py:371
  124.2 1.4 copy-start.1
  141.6 31.6 %collective-permute-start.17 = (bf16[256,768]{1,0:T(8,128)(2,1)}, bf16[256,768]{1,0:T(8,128)(2,1)}, u32[]{:S(2)}, u32[]{:S(2)}) collective-permute-start(bf16[256,768]{1,0:T(8,128)(2,1)} %get-tuple-element.46.refs_0_), channel_id=1, source_target_pairs={{0,16},{8,24},{16,0},{24,8},{1,17},{9,25},{17,1},{25,9},{2,18},{10... | collective-permute-start | bytes 1179656 | tf_op jit(solution)/shard_map/ppermute | solution.py:371
  158.3 14.9 %collective-permute-start.22 = (bf16[256,768]{1,0:T(8,128)(2,1)S(1)}, bf16[256,768]{1,0:T(8,128)(2,1)}, u32[]{:S(2)}, u32[]{:S(2)}) collective-permute-start(bf16[256,768]{1,0:T(8,128)(2,1)S(1)} %get-tuple-element.49.rest_0_.rest_2_), channel_id=1, source_target_pairs={{0,16},{8,24},{16,0},{24,8},{1,17},{9,25},{17,1},{25,9},{2,18},{10... | collective-permute-start | bytes 1179656 | tf_op jit(solution)/shard_map/ppermute | solution.py:371
  158.5 14.7 %collective-permute-start.23 = (bf16[256,768]{1,0:T(8,128)(2,1)}, bf16[256,768]{1,0:T(8,128)(2,1)}, u32[]{:S(2)}, u32[]{:S(2)}) collective-permute-start(bf16[256,768]{1,0:T(8,128)(2,1)} %get-tuple-element.50), channel_id=1, source_target_pairs={{0,8},{8,0},{16,24},{24,16},{1,9},{9,1},{17,25},{25,17},{2,10},{10... | collective-permute-start | bytes 1179656 | tf_op jit(solution)/shard_map/ppermute | solution.py:368
  159.7 16.1 %collective-permute-start.18 = (bf16[256,768]{1,0:T(8,128)(2,1)}, bf16[256,768]{1,0:T(8,128)(2,1)}, u32[]{:S(2)}, u32[]{:S(2)}) collective-permute-start(bf16[256,768]{1,0:T(8,128)(2,1)} %get-tuple-element.47), channel_id=1, source_target_pairs={{0,8},{8,0},{16,24},{24,16},{1,9},{9,1},{17,25},{25,17},{2,10},{10... | collective-permute-start | bytes 1179656 | tf_op jit(solution)/shard_map/ppermute | solution.py:368
  189.9 1.2 copy-start.6
  191.1 7.6 %collective-permute-start.26 = (bf16[6,256,768]{2,1,0:T(8,128)(2,1)}, bf16[6,256,768]{2,1,0:T(8,128)(2,1)}, u32[]{:S(2)}, u32[]{:S(2)}) collective-permute-start(bf16[6,256,768]{2,1,0:T(8,128)(2,1)} %get-tuple-element.52.s0), channel_id=1, source_target_pairs={{0,1},{1,0},{2,3},{3,2},{4,5},{5,4},{6,7},{7,6},{8,9},{9,8},{10,11... | collective-permute-start | bytes 7077896 | tf_op jit(solution)/shard_map/ppermute | solution.py:374
  195.3 3.4 %copy-start.2 = (bf16[4,256,768]{2,1,0:T(8,128)(2,1)S(1)}, bf16[4,256,768]{2,1,0:T(8,128)(2,1)}, u32[]{:S(2)}) copy-start(bf16[4,256,768]{2,1,0:T(8,128)(2,1)} %copy-done) | copy-start | bytes 4718596
  196.6 29.0 %collective-permute-start.25 = (bf16[4,256,768]{2,1,0:T(8,128)(2,1)S(1)}, bf16[4,256,768]{2,1,0:T(8,128)(2,1)S(1)}, u32[]{:S(2)}, u32[]{:S(2)}) collective-permute-start(bf16[4,256,768]{2,1,0:T(8,128)(2,1)S(1)} %constant_dynamic-update-slice_fusion.rest_1_.s0), channel_id=1, source_target_pairs={{0,1},{1,0},{2,3},{3,2},{4,5},{5,4},{6,7},{7,6},{8,9},{9,8},{10,11... | collective-permute-start | bytes 4718600 | tf_op jit(solution)/shard_map/ppermute | solution.py:374
  198.1 45.3 %collective-permute-start.24 = (bf16[2,256,768]{2,1,0:T(8,128)(2,1)S(1)}, bf16[2,256,768]{2,1,0:T(8,128)(2,1)S(1)}, u32[]{:S(2)}, u32[]{:S(2)}) collective-permute-start(bf16[2,256,768]{2,1,0:T(8,128)(2,1)S(1)} %pad_maximum_fusion.s0), channel_id=1, source_target_pairs={{0,1},{1,0},{2,3},{3,2},{4,5},{5,4},{6,7},{7,6},{8,9},{9,8},{10,11... | collective-permute-start | bytes 2359304 | tf_op jit(solution)/shard_map/ppermute | solution.py:374
Sparse Core Ops, SparseCore 0:
  9.6 59.6 all-gather.2
  70.8 63.4 all-gather.4
  194.2 31.9 reduce-scatter.1

commit v2 on v1

--- a/solution.py
+++ b/solution.py
@@ -209,40 +209,50 @@
     ]
 
 
-def hidden_body(*refs):
-    tokens, (hidden, pack, steep) = refs[6], refs[-3:]
+def activate_body(*refs):
+    cs, xs, (hidden, slope, pack) = refs[12], refs[13], refs[-3:]
     wide = hidden.shape[2]
-    for h, pre in sum_of(*refs[:6]):
-        value = gelu_value(pre).astype(jnp.bfloat16)
-        hidden[h] = pack[h] = value
-        pack[2 + h] = tokens[:, h * wide : (h + 1) * wide]
-        steep[h] = gelu_slope(pre)
-
-
-def slope_body(*refs):
-    tokens, steep, (slope, pack) = refs[6], refs[7], refs[-2:]
-    wide = slope.shape[2]
-    for h, back in sum_of(*refs[:6]):
-        value = (back * steep[h]).astype(jnp.bfloat16)
-        slope[h] = pack[h] = value
-        pack[2 + h] = tokens[:, h * wide : (h + 1) * wide]
-
-
-def finish(body, name, kinds, parts, tokens, more=(), after=()):
-    _, rows, wide = parts[0].shape
-    kept = pl.BlockSpec((None, rows, wide), lambda i: (0, 0, 0))
-    late = pl.BlockSpec((rows, wide), lambda i: (0, 0))
-    full = pl.BlockSpec((2, rows, wide), lambda i: (0, 0, 0))
-    return pl.pallas_call(
-        body,
+    for (h, pre), (_, back) in zip(sum_of(*refs[:6]), sum_of(*refs[6:12])):
+        half = slice(h * wide, (h + 1) * wide)
+        hidden[h] = pack[h] = gelu_value(pre).astype(jnp.bfloat16)
+        pack[2 + h] = cs[:, half]
+        slope[h] = pack[4 + h] = (back * gelu_slope(pre)).astype(jnp.bfloat16)
+        pack[6 + h] = xs[:, half]
+
+
+def activate(pre_parts, back_parts, c_all, x_all):
+    _, rows, wide = pre_parts[0].shape
+    part = rows // 4 if rows % 64 == 0 else rows
+    kept = pl.BlockSpec((None, part, wide), lambda i: (0, i, 0))
+    late = pl.BlockSpec((part, wide), lambda i: (i, 0))
+    return pl.pallas_call(
+        activate_body,
+        grid=(rows // part,),
+        in_specs=[kept, kept, late] * 4
+        + [pl.BlockSpec((part, c_all.shape[1]), lambda i: (i, 0))] * 2,
+        out_specs=[pl.BlockSpec((n, part, wide), lambda i: (0, i, 0)) for n in (2, 2, 8)],
+        out_shape=[jax.ShapeDtypeStruct((n, rows, wide), jnp.bfloat16) for n in (2, 2, 8)],
+        compiler_params=pltpu.CompilerParams(vmem_limit_bytes=vmem_bytes),
+        name="activate",
+    )(*pre_parts, *back_parts, c_all, x_all)
+
+
+def stack_body(far_a, far_b, *refs):
+    refs[-1][0] = far_a[...]
+    refs[-1][1] = far_b[...]
+
+
+def stack(far_a, far_b, after):
+    rows, wide = far_a.shape
+    return pl.pallas_call(
+        stack_body,
         grid=(1,),
-        in_specs=[kept, kept, late] * 2 + [pl.BlockSpec(tokens.shape, lambda i: (0, 0))]
-        + [full] * len(more) + [hbm] * len(after),
-        out_specs=[pl.BlockSpec((n, rows, wide), lambda i: (0, 0, 0)) for n, _ in kinds],
-        out_shape=[jax.ShapeDtypeStruct((n, rows, wide), k) for n, k in kinds],
-        compiler_params=pltpu.CompilerParams(vmem_limit_bytes=vmem_bytes),
-        name=name,
-    )(*parts, tokens, *more, *after)
+        in_specs=[pl.BlockSpec((rows, wide), lambda i: (0, 0))] * 2 + [hbm] * len(after),
+        out_specs=pl.BlockSpec((2, rows, wide), lambda i: (0, 0, 0)),
+        out_shape=jax.ShapeDtypeStruct((2, rows, wide), jnp.bfloat16),
+        compiler_params=pltpu.CompilerParams(vmem_limit_bytes=vmem_bytes),
+        name="stack",
+    )(far_a, far_b, *after)
 
 
 def forward_body(from_x, from_y, *refs):
@@ -306,31 +316,33 @@
             out[:, to] = total_of(v0, v1)
 
 
-def tally(kind, quarters, fixed, halves, moments, into, scale, after=()):
+def tally(kind, quarters, fixed, halves, moments, into, scale, after=(), skip=0):
     rows, cols = moments[0].shape
     n_half, (_, toks, wide) = 2 * (quarters.size - 1), halves[0].shape
     if kind == "in":
-        high = 256 if wide % 256 == 0 else wide
+        high = wide
         grid = (n_half // 2, rows // high)
         per = wide // high
         fixed_specs = [
             pl.BlockSpec((toks, high), lambda k, i, q: (0, i)),
-            pl.BlockSpec((None, toks, high), lambda k, i, q: (2 + i // per, 0, i % per)),
+            pl.BlockSpec((None, toks, high), lambda k, i, q: (6 + i // per, 0, i % per)),
         ]
-        pair_spec = pl.BlockSpec((2, toks, wide), lambda k, i, q: (k, 0, 0))
+        pair_specs = [
+            pl.BlockSpec((2, toks, wide), lambda k, i, q, b=b: (k + b, 0, 0)) for b in (0, skip)
+        ]
         m_spec = pl.BlockSpec((high, 2 * wide), lambda k, i, q: (i, q[k]))
         peer_spec = pl.BlockSpec((None, high, 2 * wide), lambda k, i, q: (q[n_half // 2], i, q[k]))
         body = functools.partial(tally_in_body, scale)
         area = rows * n_half * wide
     else:
-        high = 256 if wide % 256 == 0 else wide
+        high = wide
         per = wide // high
         grid = (n_half // 2, 2, per)
         fixed_specs = [
             pl.BlockSpec((toks, cols), lambda k, h, i, q: (0, 0)),
             pl.BlockSpec((2, toks, wide), lambda k, h, i, q: (1, 0, 0)),
         ]
-        pair_spec = pl.BlockSpec((None, toks, high), lambda k, h, i, q: (2 * k + h, 0, i))
+        pair_specs = [pl.BlockSpec((None, toks, high), lambda k, h, i, q: (2 * k + h, 0, i))] * 2
         m_spec = pl.BlockSpec((high, cols), lambda k, h, i, q: ((2 * q[k] + h) * per + i, 0))
         peer_spec = pl.BlockSpec(
             (None, high, cols), lambda k, h, i, q: (q[n_half // 2], (2 * q[k] + h) * per + i, 0)
@@ -343,7 +355,7 @@
         grid_spec=pltpu.PrefetchScalarGridSpec(
             num_scalar_prefetch=1,
             grid=grid,
-            in_specs=fixed_specs + [pair_spec] * 2
+            in_specs=fixed_specs + pair_specs
             + [m_spec, peer_spec if moments[1].ndim == 3 else m_spec]
             + [hbm] * len(old + list(after)),
             out_specs=m_spec,
@@ -358,6 +370,8 @@
 
 def shards_square(n_col, n_rep, patches, cotangent, w_in, w_out, moment_in, moment_out):
     n_row = 4
+    if n_row * w_in.shape[0] != w_in.shape[1] or w_in.shape[0] % 256:
+        return shards_plain(patches, cotangent, w_in, w_out, moment_in, moment_out)
     across_x = [(i, i ^ 1) for i in range(n_row)]
     across_y = [(i, i ^ 2) for i in range(n_row)]
     swap = [(0, 1), (1, 0)]
@@ -403,30 +417,28 @@
     late_a, late_b = late_sums(back_a, back_got_a, back_b, back_got_b, after=(late_a,))
     back_late_a, back_late_b = to_y(late_a), to_x(late_b)
 
-    bf16 = jnp.bfloat16
-    hidden, pack, steep = finish(
-        hidden_body, "hidden", ((2, bf16), (4, bf16), (2, jnp.float32)),
-        (pre_a, pre_got_a, pre_late_a, pre_b, pre_got_b, pre_late_b), c_all, after=(late_a,),
-    )
-    hidden_x, hidden_y, hidden_other = to_x(hidden), to_y(hidden), other(pack)
-    slope, pack = finish(
-        slope_body, "slope", ((2, bf16), (4, bf16)),
-        (back_a, back_got_a, back_late_a, back_b, back_got_b, back_late_b), x_all, (steep,),
-    )
-    slope_x, slope_y, slope_other = to_x(slope), to_y(slope), other(pack)
-
-    both_c, both_out = (c_all, hidden_other), (moment_out, every_moment_out)
-    both_x, both_in = (x_all, slope_other), (moment_in, every_moment_in)
+    hidden, slope, pack = activate(
+        (pre_a, pre_got_a, pre_late_a, pre_b, pre_got_b, pre_late_b),
+        (back_a, back_got_a, back_late_a, back_b, back_got_b, back_late_b),
+        c_all,
+        x_all,
+    )
+    pack = other(pack)
+    hidden_x, hidden_y = to_x(hidden), to_y(hidden)
+    slope_x, slope_y = to_x(slope), to_y(slope)
+
+    both_c, both_out = (c_all, pack), (moment_out, every_moment_out)
+    both_x, both_in = (x_all, pack), (moment_in, every_moment_in)
 
     tally_out = tally(
-        "out", quarters(0), both_c, (hidden, hidden_other), both_out, None, scale, after=(slope,)
+        "out", quarters(0), both_c, (hidden, pack), both_out, None, scale
     )
     near_a, near_b = forward(hidden_x, hidden_y, after=(tally_out,))
     hidden_far_a, hidden_far_b = to_y(near_a), to_x(near_b)
-    far_a, far_b = forward(slope_x, slope_y, after=(near_a,))
     tally_in = tally(
-        "in", quarters(0), both_x, (slope, slope_other), both_in, None, scale, after=(far_a,)
-    )
+        "in", quarters(0), both_x, (slope, pack), both_in, None, scale, after=(near_a,), skip=2
+    )
+    far_a, far_b = forward(slope_x, slope_y, after=(tally_in,))
     slope_far_a, slope_far_b = to_y(far_a), to_x(far_b)
     column = jnp.reshape(lax.axis_index("col"), (1,)).astype(jnp.int32)
     parts, hidden_rest = mix(
@@ -435,9 +447,9 @@
         + [(hidden_far_a, 0), (hidden_far_b, 0)],
         w_out,
         n_col,
-        after=(tally_in, slope_far_a, slope_far_b),
-    )
-    mixed = lax.psum_scatter(parts, "col", scatter_dimension=0, tiled=True).astype(bf16)
+        after=(far_a,),
+    )
+    mixed = lax.psum_scatter(parts, "col", scatter_dimension=0, tiled=True).astype(jnp.bfloat16)
     hidden_rest_other = other(hidden_rest)
     near = jnp.concatenate([slope_x, slope_y])
     near_other = other(near)
@@ -445,11 +457,11 @@
         "out", quarters(1, 2, 3), both_c, (hidden_rest, hidden_rest_other), both_out, tally_out,
         scale, after=(near, far_a),
     )
+    far = stack(slope_far_a, slope_far_b, after=(tally_out,))
     tally_in = tally(
         "in", quarters(1, 2), both_x, (near, near_other), both_in, tally_in, scale,
-        after=(tally_out,),
-    )
-    far = jnp.stack([slope_far_a, slope_far_b])
+        after=(tally_out, far),
+    )
     tally_in = tally("in", quarters(3), both_x, (far, other(far)), both_in, tally_in, scale)
     return mixed, tally_in, tally_out
 

time: 264 us -> 239 us (0.905)
  Pallas kernels: 131 us -> 119 us
  waiting for transfers between devices: 81.9 us -> 70 us
    ppermute x8, waiting for transfers between devices: 37.7 us -> 17.5 us  [to_x(): return lax.ppermute(a, 'row', across_x)]
    pallas_call x5, Pallas kernels: 75.2 us -> 63.9 us  [tally(): pl.pallas_call(body, grid_spec=pltpu.PrefetchScalarGridSpec(num_scalar_pr...]
    ppermute x5 -> x4, waiting for transfers between devices: 0.01 us -> 6.99 us  [other(): return lax.ppermute(a, 'rep', swap)]
    ppermute x5 -> x4, starting transfers between devices: 6.51 us -> 3.55 us  [other(): return lax.ppermute(a, 'rep', swap)]
    unnamed x19 -> x39, local copies, waits for them, and re-layouts: 5.02 us -> 7.4 us
  transfers between devices with their start and end apart: 30 -> 29, of which waited for: 13 -> 11; matrix products, arithmetic and copies ran while one was open for 2% -> 2% of each run, Pallas kernels for 45% -> 40%
where the time goes in v2:
time: 239 us; the launch traced here: 238 us
  Pallas kernels  119 us (50%)
  waiting for transfers between devices  70 us (29%)
  starting transfers between devices  25.1 us (11%)
  between operations  13.9 us (6%)
  local copies, waits for them, and re-layouts  8.58 us (4%)
    pallas_call x5, Pallas kernels, tally(): pl.pallas_call(body, grid_spec=pltpu.PrefetchScalarGridSpec(num_scalar_pr...  63.9 us
    pallas_call x2, Pallas kernels, project(): pl.pallas_call(functools.partial(project_body, transposed, len(toks)), gr...  28.6 us
    ppermute x8, waiting for transfers between devices, to_y(): return lax.ppermute(a, 'row', across_y)  23.4 us
    ppermute x6, waiting for transfers between devices, along(): lax.ppermute(a, 'col', [(i, (i + shift) % n_col) for i in range(n_col)])  20.7 us
    ppermute x8, waiting for transfers between devices, to_x(): return lax.ppermute(a, 'row', across_x)  17.5 us
    pallas_call x1, Pallas kernels, mix(): pl.pallas_call(functools.partial(mix_body, n_half, n_col, len(after)), gr...  14.4 us
    ppermute x8, starting transfers between devices, to_y(): return lax.ppermute(a, 'row', across_y)  8.21 us
    ppermute x6, starting transfers between devices, along(): lax.ppermute(a, 'col', [(i, (i + shift) % n_col) for i in range(n_col)])  8.15 us
  transfers between devices with their start and end apart: 29, of which 11 were waited for; matrix products, arithmetic and copies ran while one was open for 2% of the time, Pallas kernels for 40%

profile of v2, /device:TPU:9, one launch (start us, length us, event | category | flops | bytes accessed | tf_op | source)
XLA Modules:
  0.0 238.4 jit_solution(12552201909191123251)
XLA Ops:
  8.8 1.3 collective-permute-start
  10.1 1.0 collective-permute-start.1
  11.2 1.4 collective-permute-start.2
  12.6 3.2 %collective-permute-start.6 = (bf16[64,1536]{1,0:T(8,128)(2,1)S(1)}, bf16[64,1536]{1,0:T(8,128)(2,1)S(1)}, u32[]{:S(2)}, u32[]{:S(2)}) collective-permute-start(bf16[64,1536]{1,0:T(8,128)(2,1)S(1)} %bitcast.12), channel_id=1, source_target_pairs={{0,4},{2,6},{4,0},{6,2},{1,5},{3,7},{5,1},{7,3},{8,12},{10,14},{12... | collective-permute-start | bytes 589832 | tf_op jit(solution)/shard_map/ppermute | solution.py:391
  15.8 1.2 collective-permute-start.7
  17.0 9.4 %collective-permute-done.1.refs_2_ = bf16[64,1536]{1,0:T(8,128)(2,1)S(1)} collective-permute-done((bf16[64,1536]{1,0:T(8,128)(2,1)S(1)}, bf16[64,1536]{1,0:T(8,128)(2,1)S(1)}, u32[]{:S(2)}, u32[]{:S(2)}) %collective-permute-start.1) | collective-permute-done | bytes 196640 | tf_op jit(solution)/shard_map/ppermute | solution.py:391
  26.4 11.3 %collective-permute-done.2.refs_3_ = bf16[64,1536]{1,0:T(8,128)(2,1)S(1)} collective-permute-done((bf16[64,1536]{1,0:T(8,128)(2,1)S(1)}, bf16[64,1536]{1,0:T(8,128)(2,1)S(1)}, u32[]{:S(2)}, u32[]{:S(2)}) %collective-permute-start.2) | collective-permute-done | bytes 196640 | tf_op jit(solution)/shard_map/ppermute | solution.py:391
  37.6 15.7 %project_pre.1 = (bf16[2,256,768]{2,1,0:T(8,128)(2,1)S(1)}, f32[2,256,768]{2,1,0:T(8,128)S(1)}, bf16[2,256,768]{2,1,0:T(8,128)(2,1)S(1)}, f32[2,256,768]{2,1,0:T(8,128)}, bf16[256,1536]{1,0:T(8,128)(2,1)S(1)}) custom-call(s32[1]{0:T(128)} %bitcast.idx, bf16[64,1536]{1,0:T(8,128)(2,1)S(1)} %bitcast.10, bf16[64,1536]{1,0:T(8,128)(2,1)S(1)} %collective-permute-done.refs_1_, ...), custom_call_target="tpu_custom_call" | custom-call | flops 4831838208 | bytes 24379392 | tf_op jit(solution)/shard_map/project_pre/pallas_call | solution.py:118
  53.4 1.2 collective-permute-start.3
  54.5 1.3 collective-permute-start.4
  55.8 12.8 %project_back.1 = (bf16[2,256,768]{2,1,0:T(8,128)(2,1)S(1)}, f32[2,256,768]{2,1,0:T(8,128)S(1)}, bf16[2,256,768]{2,1,0:T(8,128)(2,1)S(1)}, f32[2,256,768]{2,1,0:T(8,128)}, bf16[256,1536]{1,0:T(8,128)(2,1)S(1)}) custom-call(s32[1]{0:T(128)} %bitcast.idx, bf16[64,1536]{1,0:T(8,128)(2,1)S(1)} %bitcast.14, bf16[64,1536]{1,0:T(8,128)(2,1)S(1)} %collective-permute-done.5.refs_1_, ...), custom_call_target="tpu_custom_call" | custom-call | flops 4831838208 | bytes 24379392 | tf_op jit(solution)/shard_map/project_back/pallas_call | solution.py:118
  69.5 2.4 %collective-permute-done.3.got_a.refs_1_ = bf16[2,256,768]{2,1,0:T(8,128)(2,1)S(1)} collective-permute-done((bf16[2,256,768]{2,1,0:T(8,128)(2,1)S(1)}, bf16[2,256,768]{2,1,0:T(8,128)(2,1)S(1)}, u32[]{:S(2)}, u32[]{:S(2)}) %collective-permute-start.3) | collective-permute-done | bytes 786464 | tf_op jit(solution)/shard_map/ppermute | solution.py:382
  71.9 0.9 collective-permute-done.4.got_b.refs_4_
  72.8 1.4 late_sums.2
  74.2 1.3 collective-permute-start.8
  75.8 13.0 %collective-permute-done.10.got_a.refs_7_ = bf16[2,256,768]{2,1,0:T(8,128)(2,1)S(1)} collective-permute-done((bf16[2,256,768]{2,1,0:T(8,128)(2,1)S(1)}, bf16[2,256,768]{2,1,0:T(8,128)(2,1)S(1)}, u32[]{:S(2)}, u32[]{:S(2)}) %collective-permute-start.10) | collective-permute-done | bytes 786464 | tf_op jit(solution)/shard_map/ppermute | solution.py:382
  88.8 0.9 collective-permute-done.11.got_b.refs_10_
  90.5 1.2 collective-permute-start.12
  92.1 6.0 %collective-permute-done.8.refs_2_ = bf16[256,768]{1,0:T(8,128)(2,1)S(1)} collective-permute-done((bf16[256,768]{1,0:T(8,128)(2,1)S(1)}, bf16[256,768]{1,0:T(8,128)(2,1)S(1)}, u32[]{:S(2)}, u32[]{:S(2)}) %collective-permute-start.8) | collective-permute-done | bytes 393248 | tf_op jit(solution)/shard_map/ppermute | solution.py:385
  98.1 8.4 %collective-permute-done.12.refs_8_ = bf16[256,768]{1,0:T(8,128)(2,1)S(1)} collective-permute-done((bf16[256,768]{1,0:T(8,128)(2,1)S(1)}, bf16[256,768]{1,0:T(8,128)(2,1)S(1)}, u32[]{:S(2)}, u32[]{:S(2)}) %collective-permute-start.12) | collective-permute-done | bytes 393248 | tf_op jit(solution)/shard_map/ppermute | solution.py:385
  106.5 6.3 %activate.1 = (bf16[2,256,768]{2,1,0:T(8,128)(2,1)}, bf16[2,256,768]{2,1,0:T(8,128)(2,1)}, bf16[8,256,768]{2,1,0:T(8,128)(2,1)}) custom-call(f32[2,256,768]{2,1,0:T(8,128)} %copy-done.9, bf16[2,256,768]{2,1,0:T(8,128)(2,1)S(1)} %collective-permute-done.3.got_a.refs_1_, bf16[256,768]{1,0:T(8,128)(2,1)S(1)} %collective-permute-done.8.refs_2_, ...), custom_call_target="tpu_custom_call" | custom-call | tf_op jit(solution)/shard_map/activate/pallas_call | solution.py:228
  112.8 1.5 collective-permute-start.16
  114.6 1.2 collective-permute-start.15
  115.8 1.1 collective-permute-start.19
  117.3 7.0 %collective-permute-done.16.c1.s1.x1 = bf16[8,256,768]{2,1,0:T(8,128)(2,1)S(1)} collective-permute-done((bf16[8,256,768]{2,1,0:T(8,128)(2,1)}, bf16[8,256,768]{2,1,0:T(8,128)(2,1)S(1)}, u32[]{:S(2)}, u32[]{:S(2)}) %collective-permute-start.16) | collective-permute-done | bytes 3145760 | tf_op jit(solution)/shard_map/ppermute | solution.py:388
  124.3 1.7 copy-done.7
  126.0 8.8 %tally_out.2.refs_0_.rest_0_ = bf16[6144,1536]{1,0:T(8,128)(2,1)} custom-call(s32[2]{0:T(128)S(1)} %pad_add_fusion.4.idx, bf16[256,1536]{1,0:T(8,128)(2,1)S(1)} %copy-done.7, bf16[8,256,768]{2,1,0:T(8,128)(2,1)S(1)} %collective-permute-done.16.c1.s1.x1, bf16[2,256,768]{2,1,0:T(8,128)(2,1)} %get-tuple-element.40.s0.refs_0_.refs_1_, ...), custom_call_target="tpu_custom_call" | custom-call | flops 2415919104 | bytes 14155776 | tf_op jit(solution)/shard_map/tally_out/pallas_call | solution.py:353
  134.8 1.9 forward.2
  136.7 1.2 collective-permute-start.17
  138.4 1.1 copy-done.3
  139.5 8.9 %tally_in.3.refs_0_.rest_0_ = bf16[1536,6144]{1,0:T(8,128)(2,1)} custom-call(s32[2]{0:T(128)S(1)} %pad_add_fusion.4.idx, bf16[256,1536]{1,0:T(8,128)(2,1)S(1)} %copy-done.3, bf16[8,256,768]{2,1,0:T(8,128)(2,1)S(1)} %collective-permute-done.16.c1.s1.x1, bf16[2,256,768]{2,1,0:T(8,128)(2,1)} %get-tuple-element.44.s0, ...), custom_call_target="tpu_custom_call" | custom-call | flops 2415919104 | bytes 14155776 | tf_op jit(solution)/shard_map/tally_in/pallas_call | solution.py:353
  148.4 2.1 collective-permute-done.19.from_x
  150.6 1.2 forward.3
  151.7 7.2 %collective-permute-done.17.refs_6_ = bf16[256,768]{1,0:T(8,128)(2,1)} collective-permute-done((bf16[256,768]{1,0:T(8,128)(2,1)S(1)}, bf16[256,768]{1,0:T(8,128)(2,1)}, u32[]{:S(2)}, u32[]{:S(2)}) %collective-permute-start.17) | collective-permute-done | bytes 393248 | tf_op jit(solution)/shard_map/ppermute | solution.py:385
  159.0 14.4 %mix.1 = (f32[4,64,1536]{2,1,0:T(8,128)S(1)}, bf16[6,256,768]{2,1,0:T(8,128)(2,1)}) custom-call(s32[2]{0:T(128)S(1)} %pad_add_fusion.idx, bf16[2,256,768]{2,1,0:T(8,128)(2,1)} %get-tuple-element.40.s0.refs_0_.refs_1_, bf16[2,256,768]{2,1,0:T(8,128)(2,1)} %get-tuple-element.40.s0.refs_0_.refs_1_, ...), custom_call_target="tpu_custom_call" | custom-call | flops 4831838208 | bytes 26738688 | tf_op jit(solution)/shard_map/mix/pallas_call | solution.py:166
  173.4 1.2 copy-done.14
  174.6 1.2 collective-permute-start.23
  175.8 1.3 constant_dynamic-update-slice_fusion.1
  177.1 1.2 constant_dynamic-update-slice_fusion.rest_1_.s0
  178.5 1.2 collective-permute-start.21
  179.7 1.1 collective-permute-start.22
  180.9 21.8 %tally_out.3.refs_0_.rest_1_ = bf16[6144,1536]{1,0:T(8,128)(2,1)} custom-call(s32[4]{0:T(128)S(1)} %pad_add_fusion.2.idx, bf16[256,1536]{1,0:T(8,128)(2,1)S(1)} %copy-done.8, bf16[8,256,768]{2,1,0:T(8,128)(2,1)} %copy-done, bf16[6,256,768]{2,1,0:T(8,128)(2,1)S(1)} %copy-done.13, ...), custom_call_target="tpu_custom_call", output_to_operand_aliasing={{}: (7, {})} | custom-call | flops 7247757312 | bytes 42467328 | tf_op jit(solution)/shard_map/tally_out/pallas_call | solution.py:353
  202.7 1.0 stack.1.rest_2_.s0
  203.7 0.8 collective-permute-start.24
  204.7 15.1 %tally_in.4.rest_0_ = bf16[1536,6144]{1,0:T(8,128)(2,1)} custom-call(s32[3]{0:T(128)S(1)} %pad_add_fusion.3.idx, bf16[256,1536]{1,0:T(8,128)(2,1)S(1)} %copy-done.4, bf16[8,256,768]{2,1,0:T(8,128)(2,1)} %copy-done, bf16[4,256,768]{2,1,0:T(8,128)(2,1)S(1)} %constant_dynamic-update-slice_fusion.rest_1_.s0, ...), custom_call_target="tpu_custom_call", output_to_operand_aliasing={{}: (7, {})} | custom-call | flops 4831838208 | bytes 28311552 | tf_op jit(solution)/shard_map/tally_in/pallas_call | solution.py:353
  219.8 1.7 convert_element_type.3
  221.5 1.1 copy-done.5
  222.6 9.2 %tally_in.5 = bf16[1536,6144]{1,0:T(8,128)(2,1)} custom-call(s32[2]{0:T(128)S(1)} %pad_add_fusion.1.idx, bf16[256,1536]{1,0:T(8,128)(2,1)S(1)} %copy-done.5, bf16[8,256,768]{2,1,0:T(8,128)(2,1)S(1)} %copy-done.1, bf16[2,256,768]{2,1,0:T(8,128)(2,1)} %stack.1.rest_2_.s0, ...), custom_call_target="tpu_custom_call", output_to_operand_aliasing={{}: (7, {})} | custom-call | flops 2415919104 | bytes 14155776 | tf_op jit(solution)/shard_map/tally_in/pallas_call | solution.py:353
  (73 shorter events, 5.5 us)
Async XLA Ops:
  7.2 117.1 %all-gather.3.cloned.1.call-start = ((), (), s32[]{:S(2)}) async-start(), calls=%async_computation.1 | async-start | bytes 56623104 | tf_op jit(solution)/shard_map/all_gather | solution.py:406
  7.9 0.9 copy-start.15
  7.9 4.7 %copy-start.16 = (bf16[1,64,1536]{2,1,0:T(8,128)(2,1)S(1)}, bf16[1,64,1536]{2,1,0:T(8,128)(2,1)}, u32[]{:S(2)}) copy-start(bf16[1,64,1536]{2,1,0:T(8,128)(2,1)} %param.7) | copy-start | bytes 589828
  7.9 130.4 %all-gather.5.cloned.1.call-start = ((), (), s32[]{:S(2)}) async-start(), calls=%async_computation.2 | async-start | bytes 56623104 | tf_op jit(solution)/shard_map/all_gather | solution.py:407
  8.7 211.1 %reduce-scatter.2.cloned.1.call-start = ((), (), s32[]{:S(2)}) async-start(), calls=%async_computation.3 | async-start | bytes 1966080 | tf_op jit(solution)/shard_map/reduce_scatter | solution.py:452
  8.8 7.0 %collective-permute-start = (bf16[64,1536]{1,0:T(8,128)(2,1)S(1)}, bf16[64,1536]{1,0:T(8,128)(2,1)S(1)}, u32[]{:S(2)}, u32[]{:S(2)}) collective-permute-start(bf16[64,1536]{1,0:T(8,128)(2,1)S(1)} %bitcast.7), channel_id=1, source_target_pairs={{0,2},{2,4},{4,6},{6,0},{1,3},{3,5},{5,7},{7,1},{8,10},{10,12},{12... | collective-permute-start | bytes 589832 | tf_op jit(solution)/shard_map/ppermute | solution.py:391
  10.1 16.3 %collective-permute-start.1 = (bf16[64,1536]{1,0:T(8,128)(2,1)S(1)}, bf16[64,1536]{1,0:T(8,128)(2,1)S(1)}, u32[]{:S(2)}, u32[]{:S(2)}) collective-permute-start(bf16[64,1536]{1,0:T(8,128)(2,1)S(1)} %bitcast.8), channel_id=1, source_target_pairs={{0,4},{2,6},{4,0},{6,2},{1,5},{3,7},{5,1},{7,3},{8,12},{10,14},{12... | collective-permute-start | bytes 589832 | tf_op jit(solution)/shard_map/ppermute | solution.py:391
  11.2 26.5 %collective-permute-start.2 = (bf16[64,1536]{1,0:T(8,128)(2,1)S(1)}, bf16[64,1536]{1,0:T(8,128)(2,1)S(1)}, u32[]{:S(2)}, u32[]{:S(2)}) collective-permute-start(bf16[64,1536]{1,0:T(8,128)(2,1)S(1)} %bitcast.9), channel_id=1, source_target_pairs={{0,6},{2,0},{4,2},{6,4},{1,7},{3,1},{5,3},{7,5},{8,14},{10,8},{12,... | collective-permute-start | bytes 589832 | tf_op jit(solution)/shard_map/ppermute | solution.py:391
  12.6 43.2 %collective-permute-start.5 = (bf16[64,1536]{1,0:T(8,128)(2,1)S(1)}, bf16[64,1536]{1,0:T(8,128)(2,1)S(1)}, u32[]{:S(2)}, u32[]{:S(2)}) collective-permute-start(bf16[64,1536]{1,0:T(8,128)(2,1)S(1)} %bitcast.11), channel_id=1, source_target_pairs={{0,2},{2,4},{4,6},{6,0},{1,3},{3,5},{5,7},{7,1},{8,10},{10,12},{12... | collective-permute-start | bytes 589832 | tf_op jit(solution)/shard_map/ppermute | solution.py:391
  12.6 43.2 %collective-permute-start.6 = (bf16[64,1536]{1,0:T(8,128)(2,1)S(1)}, bf16[64,1536]{1,0:T(8,128)(2,1)S(1)}, u32[]{:S(2)}, u32[]{:S(2)}) collective-permute-start(bf16[64,1536]{1,0:T(8,128)(2,1)S(1)} %bitcast.12), channel_id=1, source_target_pairs={{0,4},{2,6},{4,0},{6,2},{1,5},{3,7},{5,1},{7,3},{8,12},{10,14},{12... | collective-permute-start | bytes 589832 | tf_op jit(solution)/shard_map/ppermute | solution.py:391
  15.8 40.0 %collective-permute-start.7 = (bf16[64,1536]{1,0:T(8,128)(2,1)S(1)}, bf16[64,1536]{1,0:T(8,128)(2,1)S(1)}, u32[]{:S(2)}, u32[]{:S(2)}) collective-permute-start(bf16[64,1536]{1,0:T(8,128)(2,1)S(1)} %bitcast.13), channel_id=1, source_target_pairs={{0,6},{2,0},{4,2},{6,4},{1,7},{3,1},{5,3},{7,5},{8,14},{10,8},{12,... | collective-permute-start | bytes 589832 | tf_op jit(solution)/shard_map/ppermute | solution.py:391
  53.4 15.3 %copy-start.2 = (bf16[256,1536]{1,0:T(8,128)(2,1)}, bf16[256,1536]{1,0:T(8,128)(2,1)S(1)}, u32[]{:S(2)}) copy-start(bf16[256,1536]{1,0:T(8,128)(2,1)S(1)} %get-tuple-element.30.refs_5_.refs_13_.x0) | copy-start | bytes 2359300
  53.4 19.4 %copy-start.9 = (f32[2,256,768]{2,1,0:T(8,128)}, f32[2,256,768]{2,1,0:T(8,128)S(1)}, u32[]{:S(2)}) copy-start(f32[2,256,768]{2,1,0:T(8,128)S(1)} %get-tuple-element.26.keep_a.refs_0_) | copy-start | bytes 4718596
  53.4 18.6 %collective-permute-start.3 = (bf16[2,256,768]{2,1,0:T(8,128)(2,1)S(1)}, bf16[2,256,768]{2,1,0:T(8,128)(2,1)S(1)}, u32[]{:S(2)}, u32[]{:S(2)}) collective-permute-start(bf16[2,256,768]{2,1,0:T(8,128)(2,1)S(1)} %get-tuple-element.27), channel_id=1, source_target_pairs={{0,8},{8,0},{16,24},{24,16},{1,9},{9,1},{17,25},{25,17},{2,10},{10... | collective-permute-start | bytes 2359304 | tf_op jit(solution)/shard_map/ppermute | solution.py:382
  54.5 18.2 %collective-permute-start.4 = (bf16[2,256,768]{2,1,0:T(8,128)(2,1)S(1)}, bf16[2,256,768]{2,1,0:T(8,128)(2,1)S(1)}, u32[]{:S(2)}, u32[]{:S(2)}) collective-permute-start(bf16[2,256,768]{2,1,0:T(8,128)(2,1)S(1)} %get-tuple-element.29), channel_id=1, source_target_pairs={{0,16},{8,24},{16,0},{24,8},{1,17},{9,25},{17,1},{25,9},{2,18},{10... | collective-permute-start | bytes 2359304 | tf_op jit(solution)/shard_map/ppermute | solution.py:385
  68.6 5.5 %copy-start.6 = (bf16[256,1536]{1,0:T(8,128)(2,1)}, bf16[256,1536]{1,0:T(8,128)(2,1)S(1)}, u32[]{:S(2)}) copy-start(bf16[256,1536]{1,0:T(8,128)(2,1)S(1)} %get-tuple-element.31.refs_0_.refs_12_.c0) | copy-start | bytes 2359300
  68.6 21.0 %copy-start.10 = (f32[2,256,768]{2,1,0:T(8,128)}, f32[2,256,768]{2,1,0:T(8,128)S(1)}, u32[]{:S(2)}) copy-start(f32[2,256,768]{2,1,0:T(8,128)S(1)} %get-tuple-element.34.keep_a.refs_6_) | copy-start | bytes 4718596
  68.6 20.1 %collective-permute-start.10 = (bf16[2,256,768]{2,1,0:T(8,128)(2,1)S(1)}, bf16[2,256,768]{2,1,0:T(8,128)(2,1)S(1)}, u32[]{:S(2)}, u32[]{:S(2)}) collective-permute-start(bf16[2,256,768]{2,1,0:T(8,128)(2,1)S(1)} %get-tuple-element.35), channel_id=1, source_target_pairs={{0,8},{8,0},{16,24},{24,16},{1,9},{9,1},{17,25},{25,17},{2,10},{10... | collective-permute-start | bytes 2359304 | tf_op jit(solution)/shard_map/ppermute | solution.py:382
  69.0 20.7 %collective-permute-start.11 = (bf16[2,256,768]{2,1,0:T(8,128)(2,1)S(1)}, bf16[2,256,768]{2,1,0:T(8,128)(2,1)S(1)}, u32[]{:S(2)}, u32[]{:S(2)}) collective-permute-start(bf16[2,256,768]{2,1,0:T(8,128)(2,1)S(1)} %get-tuple-element.37), channel_id=1, source_target_pairs={{0,16},{8,24},{16,0},{24,8},{1,17},{9,25},{17,1},{25,9},{2,18},{10... | collective-permute-start | bytes 2359304 | tf_op jit(solution)/shard_map/ppermute | solution.py:385
  72.8 16.9 %copy-start.11 = (f32[2,256,768]{2,1,0:T(8,128)S(1)}, f32[2,256,768]{2,1,0:T(8,128)}, u32[]{:S(2)}) copy-start(f32[2,256,768]{2,1,0:T(8,128)} %get-tuple-element.36.keep_b.refs_9_) | copy-start | bytes 4718596
  74.2 23.9 %collective-permute-start.8 = (bf16[256,768]{1,0:T(8,128)(2,1)S(1)}, bf16[256,768]{1,0:T(8,128)(2,1)S(1)}, u32[]{:S(2)}, u32[]{:S(2)}) collective-permute-start(bf16[256,768]{1,0:T(8,128)(2,1)S(1)} %get-tuple-element.32.refs_0_), channel_id=1, source_target_pairs={{0,16},{8,24},{16,0},{24,8},{1,17},{9,25},{17,1},{25,9},{2,18},{10... | collective-permute-start | bytes 1179656 | tf_op jit(solution)/shard_map/ppermute | solution.py:385
  75.5 22.6 %collective-permute-start.9 = (bf16[256,768]{1,0:T(8,128)(2,1)S(1)}, bf16[256,768]{1,0:T(8,128)(2,1)S(1)}, u32[]{:S(2)}, u32[]{:S(2)}) collective-permute-start(bf16[256,768]{1,0:T(8,128)(2,1)S(1)} %get-tuple-element.33), channel_id=1, source_target_pairs={{0,8},{8,0},{16,24},{24,16},{1,9},{9,1},{17,25},{25,17},{2,10},{10... | collective-permute-start | bytes 1179656 | tf_op jit(solution)/shard_map/ppermute | solution.py:382
  89.6 0.9 copy-start.12
  90.5 16.0 %collective-permute-start.12 = (bf16[256,768]{1,0:T(8,128)(2,1)S(1)}, bf16[256,768]{1,0:T(8,128)(2,1)S(1)}, u32[]{:S(2)}, u32[]{:S(2)}) collective-permute-start(bf16[256,768]{1,0:T(8,128)(2,1)S(1)} %get-tuple-element.38), channel_id=1, source_target_pairs={{0,16},{8,24},{16,0},{24,8},{1,17},{9,25},{17,1},{25,9},{2,18},{10... | collective-permute-start | bytes 1179656 | tf_op jit(solution)/shard_map/ppermute | solution.py:385
  91.7 14.7 %collective-permute-start.13 = (bf16[256,768]{1,0:T(8,128)(2,1)S(1)}, bf16[256,768]{1,0:T(8,128)(2,1)S(1)}, u32[]{:S(2)}, u32[]{:S(2)}) collective-permute-start(bf16[256,768]{1,0:T(8,128)(2,1)S(1)} %get-tuple-element.39), channel_id=1, source_target_pairs={{0,8},{8,0},{16,24},{24,16},{1,9},{9,1},{17,25},{25,17},{2,10},{10... | collective-permute-start | bytes 1179656 | tf_op jit(solution)/shard_map/ppermute | solution.py:382
  112.8 11.5 %collective-permute-start.16 = (bf16[8,256,768]{2,1,0:T(8,128)(2,1)}, bf16[8,256,768]{2,1,0:T(8,128)(2,1)S(1)}, u32[]{:S(2)}, u32[]{:S(2)}) collective-permute-start(bf16[8,256,768]{2,1,0:T(8,128)(2,1)} %get-tuple-element.41), channel_id=1, source_target_pairs={{0,1},{1,0},{2,3},{3,2},{4,5},{5,4},{6,7},{7,6},{8,9},{9,8},{10,11... | collective-permute-start | bytes 9437192 | tf_op jit(solution)/shard_map/ppermute | solution.py:388
  114.3 20.5 %collective-permute-start.14 = (bf16[2,256,768]{2,1,0:T(8,128)(2,1)}, bf16[2,256,768]{2,1,0:T(8,128)(2,1)}, u32[]{:S(2)}, u32[]{:S(2)}) collective-permute-start(bf16[2,256,768]{2,1,0:T(8,128)(2,1)} %get-tuple-element.40.s0.refs_0_.refs_1_), channel_id=1, source_target_pairs={{0,8},{8,0},{16,24},{24,16},{1,9},{9,1},{17,25},{25,17},{2,10},{10... | collective-permute-start | bytes 2359304 | tf_op jit(solution)/shard_map/ppermute | solution.py:382
  114.6 20.2 %collective-permute-start.15 = (bf16[2,256,768]{2,1,0:T(8,128)(2,1)}, bf16[2,256,768]{2,1,0:T(8,128)(2,1)}, u32[]{:S(2)}, u32[]{:S(2)}) collective-permute-start(bf16[2,256,768]{2,1,0:T(8,128)(2,1)} %get-tuple-element.40.s0.refs_0_.refs_1_), channel_id=1, source_target_pairs={{0,16},{8,24},{16,0},{24,8},{1,17},{9,25},{17,1},{25,9},{2,18},{10... | collective-permute-start | bytes 2359304 | tf_op jit(solution)/shard_map/ppermute | solution.py:385
  115.8 34.7 %collective-permute-start.19 = (bf16[2,256,768]{2,1,0:T(8,128)(2,1)}, bf16[2,256,768]{2,1,0:T(8,128)(2,1)}, u32[]{:S(2)}, u32[]{:S(2)}) collective-permute-start(bf16[2,256,768]{2,1,0:T(8,128)(2,1)} %get-tuple-element.44.s0), channel_id=1, source_target_pairs={{0,8},{8,0},{16,24},{24,16},{1,9},{9,1},{17,25},{25,17},{2,10},{10... | collective-permute-start | bytes 2359304 | tf_op jit(solution)/shard_map/ppermute | solution.py:382
  117.0 33.6 %collective-permute-start.20 = (bf16[2,256,768]{2,1,0:T(8,128)(2,1)}, bf16[2,256,768]{2,1,0:T(8,128)(2,1)}, u32[]{:S(2)}, u32[]{:S(2)}) collective-permute-start(bf16[2,256,768]{2,1,0:T(8,128)(2,1)} %get-tuple-element.44.s0), channel_id=1, source_target_pairs={{0,16},{8,24},{16,0},{24,8},{1,17},{9,25},{17,1},{25,9},{2,18},{10... | collective-permute-start | bytes 2359304 | tf_op jit(solution)/shard_map/ppermute | solution.py:385
  124.3 14.1 %copy-start = (bf16[8,256,768]{2,1,0:T(8,128)(2,1)}, bf16[8,256,768]{2,1,0:T(8,128)(2,1)S(1)}, u32[]{:S(2)}) copy-start(bf16[8,256,768]{2,1,0:T(8,128)(2,1)S(1)} %collective-permute-done.16.c1.s1.x1) | copy-start | bytes 9437188
  124.3 1.7 copy-start.7
  136.7 22.3 %collective-permute-start.17 = (bf16[256,768]{1,0:T(8,128)(2,1)S(1)}, bf16[256,768]{1,0:T(8,128)(2,1)}, u32[]{:S(2)}, u32[]{:S(2)}) collective-permute-start(bf16[256,768]{1,0:T(8,128)(2,1)S(1)} %get-tuple-element.42.rest_0_), channel_id=1, source_target_pairs={{0,16},{8,24},{16,0},{24,8},{1,17},{9,25},{17,1},{25,9},{2,18},{10... | collective-permute-start | bytes 1179656 | tf_op jit(solution)/shard_map/ppermute | solution.py:385
  138.0 21.0 %collective-permute-start.18 = (bf16[256,768]{1,0:T(8,128)(2,1)}, bf16[256,768]{1,0:T(8,128)(2,1)}, u32[]{:S(2)}, u32[]{:S(2)}) collective-permute-start(bf16[256,768]{1,0:T(8,128)(2,1)} %get-tuple-element.43), channel_id=1, source_target_pairs={{0,8},{8,0},{16,24},{24,16},{1,9},{9,1},{17,25},{25,17},{2,10},{10... | collective-permute-start | bytes 1179656 | tf_op jit(solution)/shard_map/ppermute | solution.py:382
  138.4 1.1 copy-start.3
  151.7 21.6 %copy-start.17 = (bf16[256,768]{1,0:T(8,128)(2,1)}, bf16[256,768]{1,0:T(8,128)(2,1)S(1)}, u32[]{:S(2)}) copy-start(bf16[256,768]{1,0:T(8,128)(2,1)S(1)} %get-tuple-element.47) | copy-start | bytes 1179652
  173.4 1.2 copy-start.14
  174.6 6.3 %collective-permute-start.23 = (bf16[6,256,768]{2,1,0:T(8,128)(2,1)}, bf16[6,256,768]{2,1,0:T(8,128)(2,1)}, u32[]{:S(2)}, u32[]{:S(2)}) collective-permute-start(bf16[6,256,768]{2,1,0:T(8,128)(2,1)} %get-tuple-element.48.s0), channel_id=1, source_target_pairs={{0,1},{1,0},{2,3},{3,2},{4,5},{5,4},{6,7},{7,6},{8,9},{9,8},{10,11... | collective-permute-start | bytes 7077896 | tf_op jit(solution)/shard_map/ppermute | solution.py:388
  175.7 5.1 %copy-start.8 = (bf16[256,1536]{1,0:T(8,128)(2,1)S(1)}, bf16[256,1536]{1,0:T(8,128)(2,1)}, u32[]{:S(2)}) copy-start(bf16[256,1536]{1,0:T(8,128)(2,1)} %copy-done.6) | copy-start | bytes 2359300
  175.8 5.1 %copy-start.13 = (bf16[6,256,768]{2,1,0:T(8,128)(2,1)S(1)}, bf16[6,256,768]{2,1,0:T(8,128)(2,1)}, u32[]{:S(2)}) copy-start(bf16[6,256,768]{2,1,0:T(8,128)(2,1)} %get-tuple-element.48.s0) | copy-start | bytes 7077892
  175.8 3.9 %copy-start.18 = (bf16[256,768]{1,0:T(8,128)(2,1)S(1)}, bf16[256,768]{1,0:T(8,128)(2,1)}, u32[]{:S(2)}) copy-start(bf16[256,768]{1,0:T(8,128)(2,1)} %copy-done.17) | copy-start | bytes 1179652
  178.3 26.4 %collective-permute-start.25 = (bf16[4,256,768]{2,1,0:T(8,128)(2,1)S(1)}, bf16[4,256,768]{2,1,0:T(8,128)(2,1)S(1)}, u32[]{:S(2)}, u32[]{:S(2)}) collective-permute-start(bf16[4,256,768]{2,1,0:T(8,128)(2,1)S(1)} %constant_dynamic-update-slice_fusion.rest_1_.s0), channel_id=1, source_target_pairs={{0,1},{1,0},{2,3},{3,2},{4,5},{5,4},{6,7},{7,6},{8,9},{9,8},{10,11... | collective-permute-start | bytes 4718600 | tf_op jit(solution)/shard_map/ppermute | solution.py:388
  178.5 24.2 %collective-permute-start.21 = (bf16[256,768]{1,0:T(8,128)(2,1)S(1)}, bf16[256,768]{1,0:T(8,128)(2,1)S(1)}, u32[]{:S(2)}, u32[]{:S(2)}) collective-permute-start(bf16[256,768]{1,0:T(8,128)(2,1)S(1)} %get-tuple-element.45.refs_9_.rest_2_), channel_id=1, source_target_pairs={{0,16},{8,24},{16,0},{24,8},{1,17},{9,25},{17,1},{25,9},{2,18},{10... | collective-permute-start | bytes 1179656 | tf_op jit(solution)/shard_map/ppermute | solution.py:385
  179.7 23.0 %collective-permute-start.22 = (bf16[256,768]{1,0:T(8,128)(2,1)S(1)}, bf16[256,768]{1,0:T(8,128)(2,1)S(1)}, u32[]{:S(2)}, u32[]{:S(2)}) collective-permute-start(bf16[256,768]{1,0:T(8,128)(2,1)S(1)} %copy-done.18), channel_id=1, source_target_pairs={{0,8},{8,0},{16,24},{24,16},{1,9},{9,1},{17,25},{25,17},{2,10},{10... | collective-permute-start | bytes 1179656 | tf_op jit(solution)/shard_map/ppermute | solution.py:382
  202.7 2.0 copy-start.4
  203.7 17.8 %collective-permute-start.24 = (bf16[2,256,768]{2,1,0:T(8,128)(2,1)}, bf16[2,256,768]{2,1,0:T(8,128)(2,1)}, u32[]{:S(2)}, u32[]{:S(2)}) collective-permute-start(bf16[2,256,768]{2,1,0:T(8,128)(2,1)} %stack.1.rest_2_.s0), channel_id=1, source_target_pairs={{0,1},{1,0},{2,3},{3,2},{4,5},{5,4},{6,7},{7,6},{8,9},{9,8},{10,11... | collective-permute-start | bytes 2359304 | tf_op jit(solution)/shard_map/ppermute | solution.py:388
  204.7 16.8 %copy-start.1 = (bf16[8,256,768]{2,1,0:T(8,128)(2,1)S(1)}, bf16[8,256,768]{2,1,0:T(8,128)(2,1)}, u32[]{:S(2)}) copy-start(bf16[8,256,768]{2,1,0:T(8,128)(2,1)} %copy-done) | copy-start | bytes 9437188
  221.5 1.1 copy-start.5
Sparse Core Ops, SparseCore 0:
  9.6 59.6 all-gather.2
  70.8 63.4 all-gather.4
  175.9 31.9 reduce-scatter.1

commit v3 on v2

--- a/solution.py
+++ b/solution.py
@@ -403,8 +403,8 @@
 
     xs = [own_x] + [along(own_x, b) for b in range(1, n_col)]
     cs = [own_c] + [along(own_c, b) for b in range(1, n_col)]
-    every_moment_out = lax.all_gather(moment_out, "rep")
-    every_moment_in = lax.all_gather(moment_in, "rep")
+    every_moment_out = other(moment_out)
+    every_moment_in = other(moment_in)
 
     send_a, pre_a, send_b, pre_b, x_all = project(me, xs, w_in, False, n_row)
     pre_got_a, pre_got_b = to_x(send_a), to_y(send_b)
@@ -449,7 +449,11 @@
         n_col,
         after=(far_a,),
     )
-    mixed = lax.psum_scatter(parts, "col", scatter_dimension=0, tiled=True).astype(jnp.bfloat16)
+    mixed = lax.dynamic_index_in_dim(parts, column[0], 0)
+    for b in range(1, n_col):
+        part = lax.dynamic_index_in_dim(parts, (column[0] + n_col - b) % n_col, 0)
+        mixed = mixed + f32(along(part.astype(jnp.bfloat16), -b))
+    mixed = mixed.astype(jnp.bfloat16)
     hidden_rest_other = other(hidden_rest)
     near = jnp.concatenate([slope_x, slope_y])
     near_other = other(near)

time: 239 us -> 245 us (1.025)
  waiting for transfers between devices: 70 us -> 86.7 us
  between operations: 13.9 us -> 0.79 us
  Pallas kernels: 119 us -> 114 us
  starting transfers between devices: 25.1 us -> 29.8 us
    ppermute x8, waiting for transfers between devices: 23.4 us -> 35 us  [to_y(): return lax.ppermute(a, 'row', across_y)]
    ppermute x6 -> x9, waiting for transfers between devices: 20.7 us -> 31.8 us  [along(): lax.ppermute(a, 'col', [(i, (i + shift) % n_col) for i in range(n_col)])]
    ppermute x4 -> x6, starting transfers between devices: 3.55 us -> 6.98 us  [other(): return lax.ppermute(a, 'rep', swap)]
    pallas_call x2, Pallas kernels: 28.6 us -> 25.4 us  [project(): pl.pallas_call(functools.partial(project_body, transposed, len(toks)), gr...]
    ppermute x4 -> x6, waiting for transfers between devices: 6.99 us -> 4.01 us  [other(): return lax.ppermute(a, 'rep', swap)]
    ppermute x6 -> x9, starting transfers between devices: 8.15 us -> 8.89 us  [along(): lax.ppermute(a, 'col', [(i, (i + shift) % n_col) for i in range(n_col)])]
    unnamed x39 -> x37, local copies, waits for them, and re-layouts: 7.4 us -> 6.83 us
  transfers between devices with their start and end apart: 29 -> 31, of which waited for: 11 -> 15; matrix products, arithmetic and copies ran while one was open for 2% -> 2% of each run, Pallas kernels for 40% -> 38%
where the time goes in v3:
time: 245 us; the launch traced here: 243 us
  Pallas kernels  114 us (47%)
  waiting for transfers between devices  86.7 us (35%)
  starting transfers between devices  29.8 us (12%)
  local copies, waits for them, and re-layouts  9.31 us (4%)
    pallas_call x5, Pallas kernels, tally(): pl.pallas_call(body, grid_spec=pltpu.PrefetchScalarGridSpec(num_scalar_pr...  64 us
    ppermute x8, waiting for transfers between devices, to_y(): return lax.ppermute(a, 'row', across_y)  35 us
    ppermute x9, waiting for transfers between devices, along(): lax.ppermute(a, 'col', [(i, (i + shift) % n_col) for i in range(n_col)])  31.8 us
    pallas_call x2, Pallas kernels, project(): pl.pallas_call(functools.partial(project_body, transposed, len(toks)), gr...  25.4 us
    ppermute x8, waiting for transfers between devices, to_x(): return lax.ppermute(a, 'row', across_x)  15.9 us
    pallas_call x1, Pallas kernels, mix(): pl.pallas_call(functools.partial(mix_body, n_half, n_col, len(after)), gr...  14.2 us
    ppermute x8, starting transfers between devices, to_y(): return lax.ppermute(a, 'row', across_y)  8.98 us
    ppermute x9, starting transfers between devices, along(): lax.ppermute(a, 'col', [(i, (i + shift) % n_col) for i in range(n_col)])  8.89 us
  transfers between devices with their start and end apart: 31, of which 15 were waited for; matrix products, arithmetic and copies ran while one was open for 2% of the time, Pallas kernels for 38%

profile of v3, /device:TPU:9, one launch (start us, length us, event | category | flops | bytes accessed | tf_op | source)
XLA Modules:
  0.0 242.7 jit_solution(9154420029432432743)
XLA Ops:
  1.5 1.3 collective-permute-start
  3.8 1.5 collective-permute-start.2
  5.2 2.5 %collective-permute-done.refs_1_ = bf16[64,1536]{1,0:T(8,128)(2,1)S(1)} collective-permute-done((bf16[64,1536]{1,0:T(8,128)(2,1)}, bf16[64,1536]{1,0:T(8,128)(2,1)S(1)}, u32[]{:S(2)}, u32[]{:S(2)}) %collective-permute-start) | collective-permute-done | bytes 196640 | tf_op jit(solution)/shard_map/ppermute | solution.py:391
  7.7 1.4 collective-permute-start.5
  9.1 10.4 %collective-permute-done.1.refs_2_ = bf16[64,1536]{1,0:T(8,128)(2,1)S(1)} collective-permute-done((bf16[64,1536]{1,0:T(8,128)(2,1)}, bf16[64,1536]{1,0:T(8,128)(2,1)S(1)}, u32[]{:S(2)}, u32[]{:S(2)}) %collective-permute-start.1) | collective-permute-done | bytes 196640 | tf_op jit(solution)/shard_map/ppermute | solution.py:391
  19.6 6.7 %collective-permute-done.2.refs_3_ = bf16[64,1536]{1,0:T(8,128)(2,1)S(1)} collective-permute-done((bf16[64,1536]{1,0:T(8,128)(2,1)}, bf16[64,1536]{1,0:T(8,128)(2,1)S(1)}, u32[]{:S(2)}, u32[]{:S(2)}) %collective-permute-start.2) | collective-permute-done | bytes 196640 | tf_op jit(solution)/shard_map/ppermute | solution.py:391
  27.2 12.7 %project_pre.1 = (bf16[2,256,768]{2,1,0:T(8,128)(2,1)S(1)}, f32[2,256,768]{2,1,0:T(8,128)S(1)}, bf16[2,256,768]{2,1,0:T(8,128)(2,1)S(1)}, f32[2,256,768]{2,1,0:T(8,128)}, bf16[256,1536]{1,0:T(8,128)(2,1)S(1)}) custom-call(s32[1]{0:T(128)} %bitcast.idx, bf16[64,1536]{1,0:T(8,128)(2,1)S(1)} %bitcast.10, bf16[64,1536]{1,0:T(8,128)(2,1)S(1)} %collective-permute-done.refs_1_, ...), custom_call_target="tpu_custom_call" | custom-call | flops 4831838208 | bytes 24379392 | tf_op jit(solution)/shard_map/project_pre/pallas_call | solution.py:118
  39.8 1.2 collective-permute-start.3
  41.6 12.2 %collective-permute-done.6.refs_2_ = bf16[64,1536]{1,0:T(8,128)(2,1)S(1)} collective-permute-done((bf16[64,1536]{1,0:T(8,128)(2,1)S(1)}, bf16[64,1536]{1,0:T(8,128)(2,1)S(1)}, u32[]{:S(2)}, u32[]{:S(2)}) %collective-permute-start.6) | collective-permute-done | bytes 196640 | tf_op jit(solution)/shard_map/ppermute | solution.py:391
  53.8 1.2 collective-permute-start.4
  55.1 12.8 %project_back.1 = (bf16[2,256,768]{2,1,0:T(8,128)(2,1)S(1)}, f32[2,256,768]{2,1,0:T(8,128)S(1)}, bf16[2,256,768]{2,1,0:T(8,128)(2,1)S(1)}, f32[2,256,768]{2,1,0:T(8,128)}, bf16[256,1536]{1,0:T(8,128)(2,1)S(1)}) custom-call(s32[1]{0:T(128)} %bitcast.idx, bf16[64,1536]{1,0:T(8,128)(2,1)S(1)} %bitcast.14, bf16[64,1536]{1,0:T(8,128)(2,1)S(1)} %collective-permute-done.5.refs_1_, ...), custom_call_target="tpu_custom_call" | custom-call | flops 4831838208 | bytes 24379392 | tf_op jit(solution)/shard_map/project_back/pallas_call | solution.py:118
  68.4 3.7 %collective-permute-done.4.got_b.refs_4_ = bf16[2,256,768]{2,1,0:T(8,128)(2,1)S(1)} collective-permute-done((bf16[2,256,768]{2,1,0:T(8,128)(2,1)S(1)}, bf16[2,256,768]{2,1,0:T(8,128)(2,1)S(1)}, u32[]{:S(2)}, u32[]{:S(2)}) %collective-permute-start.4) | collective-permute-done | bytes 786464 | tf_op jit(solution)/shard_map/ppermute | solution.py:385
  72.2 1.4 late_sums.2
  73.6 1.3 collective-permute-start.8
  74.9 11.0 %collective-permute-done.10.got_a.refs_7_ = bf16[2,256,768]{2,1,0:T(8,128)(2,1)S(1)} collective-permute-done((bf16[2,256,768]{2,1,0:T(8,128)(2,1)S(1)}, bf16[2,256,768]{2,1,0:T(8,128)(2,1)S(1)}, u32[]{:S(2)}, u32[]{:S(2)}) %collective-permute-start.10) | collective-permute-done | bytes 786464 | tf_op jit(solution)/shard_map/ppermute | solution.py:382
  86.2 2.8 %collective-permute-done.11.got_b.refs_10_ = bf16[2,256,768]{2,1,0:T(8,128)(2,1)S(1)} collective-permute-done((bf16[2,256,768]{2,1,0:T(8,128)(2,1)S(1)}, bf16[2,256,768]{2,1,0:T(8,128)(2,1)S(1)}, u32[]{:S(2)}, u32[]{:S(2)}) %collective-permute-start.11) | collective-permute-done | bytes 786464 | tf_op jit(solution)/shard_map/ppermute | solution.py:385
  89.9 1.2 collective-permute-start.12
  91.1 6.3 %collective-permute-done.8.refs_2_ = bf16[256,768]{1,0:T(8,128)(2,1)S(1)} collective-permute-done((bf16[256,768]{1,0:T(8,128)(2,1)S(1)}, bf16[256,768]{1,0:T(8,128)(2,1)S(1)}, u32[]{:S(2)}, u32[]{:S(2)}) %collective-permute-start.8) | collective-permute-done | bytes 393248 | tf_op jit(solution)/shard_map/ppermute | solution.py:385
  97.7 8.2 %collective-permute-done.12.refs_8_ = bf16[256,768]{1,0:T(8,128)(2,1)S(1)} collective-permute-done((bf16[256,768]{1,0:T(8,128)(2,1)S(1)}, bf16[256,768]{1,0:T(8,128)(2,1)S(1)}, u32[]{:S(2)}, u32[]{:S(2)}) %collective-permute-start.12) | collective-permute-done | bytes 393248 | tf_op jit(solution)/shard_map/ppermute | solution.py:385
  105.9 5.7 %activate.1 = (bf16[2,256,768]{2,1,0:T(8,128)(2,1)}, bf16[2,256,768]{2,1,0:T(8,128)(2,1)}, bf16[8,256,768]{2,1,0:T(8,128)(2,1)}) custom-call(f32[2,256,768]{2,1,0:T(8,128)} %copy-done.8, bf16[2,256,768]{2,1,0:T(8,128)(2,1)S(1)} %collective-permute-done.3.got_a.refs_1_, bf16[256,768]{1,0:T(8,128)(2,1)S(1)} %collective-permute-done.8.refs_2_, ...), custom_call_target="tpu_custom_call" | custom-call | tf_op jit(solution)/shard_map/activate/pallas_call | solution.py:228
  111.5 3.1 %collective-permute-start.16 = (bf16[8,256,768]{2,1,0:T(8,128)(2,1)}, bf16[8,256,768]{2,1,0:T(8,128)(2,1)S(1)}, u32[]{:S(2)}, u32[]{:S(2)}) collective-permute-start(bf16[8,256,768]{2,1,0:T(8,128)(2,1)} %get-tuple-element.41), channel_id=1, source_target_pairs={{0,1},{1,0},{2,3},{3,2},{4,5},{5,4},{6,7},{7,6},{8,9},{9,8},{10,11... | collective-permute-start | bytes 9437192 | tf_op jit(solution)/shard_map/ppermute | solution.py:388
  114.9 1.2 collective-permute-start.15
  116.1 4.0 %collective-permute-done.16.c1.s1.x1 = bf16[8,256,768]{2,1,0:T(8,128)(2,1)S(1)} collective-permute-done((bf16[8,256,768]{2,1,0:T(8,128)(2,1)}, bf16[8,256,768]{2,1,0:T(8,128)(2,1)S(1)}, u32[]{:S(2)}, u32[]{:S(2)}) %collective-permute-start.16) | collective-permute-done | bytes 3145760 | tf_op jit(solution)/shard_map/ppermute | solution.py:388
  120.4 1.2 collective-permute-start.21
  122.8 8.8 %tally_out.2.refs_0_.rest_0_ = bf16[6144,1536]{1,0:T(8,128)(2,1)} custom-call(s32[2]{0:T(128)S(1)} %pad_add_fusion.4.idx, bf16[256,1536]{1,0:T(8,128)(2,1)S(1)} %copy-done.6, bf16[8,256,768]{2,1,0:T(8,128)(2,1)S(1)} %collective-permute-done.16.c1.s1.x1, bf16[2,256,768]{2,1,0:T(8,128)(2,1)} %get-tuple-element.40.s0.refs_0_.refs_1_, ...), custom_call_target="tpu_custom_call" | custom-call | flops 2415919104 | bytes 14155776 | tf_op jit(solution)/shard_map/tally_out/pallas_call | solution.py:353
  131.6 2.4 collective-permute-done.14.from_x.refs_2_.refs_3_
  134.0 1.9 forward.2
  135.9 1.2 collective-permute-start.18
  137.2 1.1 collective-permute-start.19
  139.5 8.9 %tally_in.3.refs_0_.rest_0_ = bf16[1536,6144]{1,0:T(8,128)(2,1)} custom-call(s32[2]{0:T(128)S(1)} %pad_add_fusion.4.idx, bf16[256,1536]{1,0:T(8,128)(2,1)S(1)} %copy-done.3, bf16[8,256,768]{2,1,0:T(8,128)(2,1)S(1)} %collective-permute-done.16.c1.s1.x1, bf16[2,256,768]{2,1,0:T(8,128)(2,1)} %get-tuple-element.44.s0, ...), custom_call_target="tpu_custom_call" | custom-call | flops 2415919104 | bytes 14155776 | tf_op jit(solution)/shard_map/tally_in/pallas_call | solution.py:353
  148.5 2.4 collective-permute-done.20.from_x
  150.9 1.2 forward.3
  152.1 7.2 %collective-permute-done.18.refs_6_ = bf16[256,768]{1,0:T(8,128)(2,1)} collective-permute-done((bf16[256,768]{1,0:T(8,128)(2,1)S(1)}, bf16[256,768]{1,0:T(8,128)(2,1)}, u32[]{:S(2)}, u32[]{:S(2)}) %collective-permute-start.18) | collective-permute-done | bytes 393248 | tf_op jit(solution)/shard_map/ppermute | solution.py:385
  159.3 14.2 %mix.1 = (f32[4,64,1536]{2,1,0:T(8,128)S(1)}, bf16[6,256,768]{2,1,0:T(8,128)(2,1)}) custom-call(s32[2]{0:T(128)S(1)} %pad_add_fusion.idx, bf16[2,256,768]{2,1,0:T(8,128)(2,1)} %get-tuple-element.40.s0.refs_0_.refs_1_, bf16[2,256,768]{2,1,0:T(8,128)(2,1)} %get-tuple-element.40.s0.refs_0_.refs_1_, ...), custom_call_target="tpu_custom_call" | custom-call | flops 4831838208 | bytes 26738688 | tf_op jit(solution)/shard_map/mix/pallas_call | solution.py:166
  173.5 1.2 collective-permute-start.28
  174.8 1.2 constant_dynamic-update-slice_fusion.1
  176.0 1.2 constant_dynamic-update-slice_fusion.rest_1_.s0
  177.8 1.3 collective-permute-start.26
  179.2 1.2 collective-permute-start.27
  180.4 1.3 dynamic-slice_convert_fusion.2
  181.8 6.7 %collective-permute-done.26.far_a = bf16[256,768]{1,0:T(8,128)(2,1)S(1)} collective-permute-done((bf16[256,768]{1,0:T(8,128)(2,1)S(1)}, bf16[256,768]{1,0:T(8,128)(2,1)S(1)}, u32[]{:S(2)}, u32[]{:S(2)}) %collective-permute-start.26) | collective-permute-done | bytes 393248 | tf_op jit(solution)/shard_map/ppermute | solution.py:385
  188.5 3.1 %collective-permute-start.24 = (bf16[1,64,1536]{2,1,0:T(8,128)(2,1)S(1)}, bf16[1,64,1536]{2,1,0:T(8,128)(2,1)S(1)}, u32[]{:S(2)}, u32[]{:S(2)}) collective-permute-start(bf16[1,64,1536]{2,1,0:T(8,128)(2,1)S(1)} %get-tuple-element.51), channel_id=1, source_target_pairs={{0,4},{2,6},{4,0},{6,2},{1,5},{3,7},{5,1},{7,3},{8,12},{10,14},{12... | collective-permute-start | bytes 589832 | tf_op jit(solution)/shard_map/ppermute | solution.py:391
  191.6 1.7 copy-done.12
  193.3 21.5 %tally_out.3.refs_0_.rest_1_ = bf16[6144,1536]{1,0:T(8,128)(2,1)} custom-call(s32[4]{0:T(128)S(1)} %pad_add_fusion.2.idx, bf16[256,1536]{1,0:T(8,128)(2,1)S(1)} %copy-done.7, bf16[8,256,768]{2,1,0:T(8,128)(2,1)} %copy-done, bf16[6,256,768]{2,1,0:T(8,128)(2,1)S(1)} %copy-done.12, ...), custom_call_target="tpu_custom_call", output_to_operand_aliasing={{}: (7, {})} | custom-call | flops 7247757312 | bytes 42467328 | tf_op jit(solution)/shard_map/tally_out/pallas_call | solution.py:353
  214.8 1.2 collective-permute-start.29
  216.1 1.8 add_convert_fusion
  217.9 16.1 %tally_in.4.rest_0_ = bf16[1536,6144]{1,0:T(8,128)(2,1)} custom-call(s32[3]{0:T(128)S(1)} %pad_add_fusion.3.idx, bf16[256,1536]{1,0:T(8,128)(2,1)S(1)} %copy-done.4, bf16[8,256,768]{2,1,0:T(8,128)(2,1)} %copy-done, bf16[4,256,768]{2,1,0:T(8,128)(2,1)S(1)} %constant_dynamic-update-slice_fusion.rest_1_.s0, ...), custom_call_target="tpu_custom_call", output_to_operand_aliasing={{}: (7, {})} | custom-call | flops 4831838208 | bytes 28311552 | tf_op jit(solution)/shard_map/tally_in/pallas_call | solution.py:353
  234.0 8.7 %tally_in.5 = bf16[1536,6144]{1,0:T(8,128)(2,1)} custom-call(s32[2]{0:T(128)S(1)} %pad_add_fusion.1.idx, bf16[256,1536]{1,0:T(8,128)(2,1)S(1)} %copy-done.4, bf16[8,256,768]{2,1,0:T(8,128)(2,1)S(1)} %copy-done.1, bf16[2,256,768]{2,1,0:T(8,128)(2,1)S(1)} %stack.1.rest_2_.s0, ...), custom_call_target="tpu_custom_call", output_to_operand_aliasing={{}: (7, {})} | custom-call | flops 2415919104 | bytes 14155776 | tf_op jit(solution)/shard_map/tally_in/pallas_call | solution.py:353
  (73 shorter events, 9.3 us)
Async XLA Ops:
  0.6 119.8 %collective-permute-start.17 = (bf16[6144,1536]{1,0:T(8,128)(2,1)}, bf16[6144,1536]{1,0:T(8,128)(2,1)}, u32[]{:S(2)}, u32[]{:S(2)}) collective-permute-start(bf16[6144,1536]{1,0:T(8,128)(2,1)} %bitcast.19), channel_id=1, source_target_pairs={{0,1},{1,0},{2,3},{3,2},{4,5},{5,4},{6,7},{7,6},{8,9},{9,8},{10,11... | collective-permute-start | bytes 56623112 | tf_op jit(solution)/shard_map/ppermute | solution.py:388
  1.4 137.0 %collective-permute-start.22 = (bf16[1536,6144]{1,0:T(8,128)(2,1)}, bf16[1536,6144]{1,0:T(8,128)(2,1)}, u32[]{:S(2)}, u32[]{:S(2)}) collective-permute-start(bf16[1536,6144]{1,0:T(8,128)(2,1)} %bitcast.15), channel_id=1, source_target_pairs={{0,1},{1,0},{2,3},{3,2},{4,5},{5,4},{6,7},{7,6},{8,9},{9,8},{10,11... | collective-permute-start | bytes 56623112 | tf_op jit(solution)/shard_map/ppermute | solution.py:388
  1.5 6.3 %collective-permute-start = (bf16[64,1536]{1,0:T(8,128)(2,1)}, bf16[64,1536]{1,0:T(8,128)(2,1)S(1)}, u32[]{:S(2)}, u32[]{:S(2)}) collective-permute-start(bf16[64,1536]{1,0:T(8,128)(2,1)} %bitcast.7), channel_id=1, source_target_pairs={{0,2},{2,4},{4,6},{6,0},{1,3},{3,5},{5,7},{7,1},{8,10},{10,12},{12... | collective-permute-start | bytes 589832 | tf_op jit(solution)/shard_map/ppermute | solution.py:391
  2.8 16.8 %collective-permute-start.1 = (bf16[64,1536]{1,0:T(8,128)(2,1)}, bf16[64,1536]{1,0:T(8,128)(2,1)S(1)}, u32[]{:S(2)}, u32[]{:S(2)}) collective-permute-start(bf16[64,1536]{1,0:T(8,128)(2,1)} %bitcast.8), channel_id=1, source_target_pairs={{0,4},{2,6},{4,0},{6,2},{1,5},{3,7},{5,1},{7,3},{8,12},{10,14},{12... | collective-permute-start | bytes 589832 | tf_op jit(solution)/shard_map/ppermute | solution.py:391
  3.8 22.5 %collective-permute-start.2 = (bf16[64,1536]{1,0:T(8,128)(2,1)}, bf16[64,1536]{1,0:T(8,128)(2,1)S(1)}, u32[]{:S(2)}, u32[]{:S(2)}) collective-permute-start(bf16[64,1536]{1,0:T(8,128)(2,1)} %bitcast.9), channel_id=1, source_target_pairs={{0,6},{2,0},{4,2},{6,4},{1,7},{3,1},{5,3},{7,5},{8,14},{10,8},{12,... | collective-permute-start | bytes 589832 | tf_op jit(solution)/shard_map/ppermute | solution.py:391
  7.7 33.3 %collective-permute-start.5 = (bf16[64,1536]{1,0:T(8,128)(2,1)}, bf16[64,1536]{1,0:T(8,128)(2,1)S(1)}, u32[]{:S(2)}, u32[]{:S(2)}) collective-permute-start(bf16[64,1536]{1,0:T(8,128)(2,1)} %bitcast.11), channel_id=1, source_target_pairs={{0,2},{2,4},{4,6},{6,0},{1,3},{3,5},{5,7},{7,1},{8,10},{10,12},{12... | collective-permute-start | bytes 589832 | tf_op jit(solution)/shard_map/ppermute | solution.py:391
  26.2 0.9 copy-start.14
  27.2 13.9 %copy-start.15 = (bf16[1,64,1536]{2,1,0:T(8,128)(2,1)S(1)}, bf16[1,64,1536]{2,1,0:T(8,128)(2,1)}, u32[]{:S(2)}) copy-start(bf16[1,64,1536]{2,1,0:T(8,128)(2,1)} %param.7) | copy-start | bytes 589828
  39.8 28.0 %copy-start.2 = (bf16[256,1536]{1,0:T(8,128)(2,1)}, bf16[256,1536]{1,0:T(8,128)(2,1)S(1)}, u32[]{:S(2)}) copy-start(bf16[256,1536]{1,0:T(8,128)(2,1)S(1)} %get-tuple-element.30.refs_5_.refs_13_.x0) | copy-start | bytes 2359300
  39.8 32.3 %copy-start.8 = (f32[2,256,768]{2,1,0:T(8,128)}, f32[2,256,768]{2,1,0:T(8,128)S(1)}, u32[]{:S(2)}) copy-start(f32[2,256,768]{2,1,0:T(8,128)S(1)} %get-tuple-element.26.keep_a.refs_0_) | copy-start | bytes 4718596
  39.8 28.3 %collective-permute-start.3 = (bf16[2,256,768]{2,1,0:T(8,128)(2,1)S(1)}, bf16[2,256,768]{2,1,0:T(8,128)(2,1)S(1)}, u32[]{:S(2)}, u32[]{:S(2)}) collective-permute-start(bf16[2,256,768]{2,1,0:T(8,128)(2,1)S(1)} %get-tuple-element.27), channel_id=1, source_target_pairs={{0,8},{8,0},{16,24},{24,16},{1,9},{9,1},{17,25},{25,17},{2,10},{10... | collective-permute-start | bytes 2359304 | tf_op jit(solution)/shard_map/ppermute | solution.py:382
  41.1 12.8 %collective-permute-start.6 = (bf16[64,1536]{1,0:T(8,128)(2,1)S(1)}, bf16[64,1536]{1,0:T(8,128)(2,1)S(1)}, u32[]{:S(2)}, u32[]{:S(2)}) collective-permute-start(bf16[64,1536]{1,0:T(8,128)(2,1)S(1)} %bitcast.12), channel_id=1, source_target_pairs={{0,4},{2,6},{4,0},{6,2},{1,5},{3,7},{5,1},{7,3},{8,12},{10,14},{12... | collective-permute-start | bytes 589832 | tf_op jit(solution)/shard_map/ppermute | solution.py:391
  41.1 14.0 %collective-permute-start.7 = (bf16[64,1536]{1,0:T(8,128)(2,1)S(1)}, bf16[64,1536]{1,0:T(8,128)(2,1)S(1)}, u32[]{:S(2)}, u32[]{:S(2)}) collective-permute-start(bf16[64,1536]{1,0:T(8,128)(2,1)S(1)} %bitcast.13), channel_id=1, source_target_pairs={{0,6},{2,0},{4,2},{6,4},{1,7},{3,1},{5,3},{7,5},{8,14},{10,8},{12,... | collective-permute-start | bytes 589832 | tf_op jit(solution)/shard_map/ppermute | solution.py:391
  53.8 18.3 %collective-permute-start.4 = (bf16[2,256,768]{2,1,0:T(8,128)(2,1)S(1)}, bf16[2,256,768]{2,1,0:T(8,128)(2,1)S(1)}, u32[]{:S(2)}, u32[]{:S(2)}) collective-permute-start(bf16[2,256,768]{2,1,0:T(8,128)(2,1)S(1)} %get-tuple-element.29), channel_id=1, source_target_pairs={{0,16},{8,24},{16,0},{24,8},{1,17},{9,25},{17,1},{25,9},{2,18},{10... | collective-permute-start | bytes 2359304 | tf_op jit(solution)/shard_map/ppermute | solution.py:385
  67.9 5.7 %copy-start.5 = (bf16[256,1536]{1,0:T(8,128)(2,1)}, bf16[256,1536]{1,0:T(8,128)(2,1)S(1)}, u32[]{:S(2)}) copy-start(bf16[256,1536]{1,0:T(8,128)(2,1)S(1)} %get-tuple-element.31.refs_0_.refs_12_.c0) | copy-start | bytes 2359300
  67.9 21.2 %copy-start.9 = (f32[2,256,768]{2,1,0:T(8,128)}, f32[2,256,768]{2,1,0:T(8,128)S(1)}, u32[]{:S(2)}) copy-start(f32[2,256,768]{2,1,0:T(8,128)S(1)} %get-tuple-element.34.keep_a.refs_6_) | copy-start | bytes 4718596
  67.9 18.1 %collective-permute-start.10 = (bf16[2,256,768]{2,1,0:T(8,128)(2,1)S(1)}, bf16[2,256,768]{2,1,0:T(8,128)(2,1)S(1)}, u32[]{:S(2)}, u32[]{:S(2)}) collective-permute-start(bf16[2,256,768]{2,1,0:T(8,128)(2,1)S(1)} %get-tuple-element.35), channel_id=1, source_target_pairs={{0,8},{8,0},{16,24},{24,16},{1,9},{9,1},{17,25},{25,17},{2,10},{10... | collective-permute-start | bytes 2359304 | tf_op jit(solution)/shard_map/ppermute | solution.py:382
  68.2 20.8 %collective-permute-start.11 = (bf16[2,256,768]{2,1,0:T(8,128)(2,1)S(1)}, bf16[2,256,768]{2,1,0:T(8,128)(2,1)S(1)}, u32[]{:S(2)}, u32[]{:S(2)}) collective-permute-start(bf16[2,256,768]{2,1,0:T(8,128)(2,1)S(1)} %get-tuple-element.37), channel_id=1, source_target_pairs={{0,16},{8,24},{16,0},{24,8},{1,17},{9,25},{17,1},{25,9},{2,18},{10... | collective-permute-start | bytes 2359304 | tf_op jit(solution)/shard_map/ppermute | solution.py:385
  72.2 16.9 %copy-start.10 = (f32[2,256,768]{2,1,0:T(8,128)S(1)}, f32[2,256,768]{2,1,0:T(8,128)}, u32[]{:S(2)}) copy-start(f32[2,256,768]{2,1,0:T(8,128)} %get-tuple-element.36.keep_b.refs_9_) | copy-start | bytes 4718596
  73.6 23.9 %collective-permute-start.8 = (bf16[256,768]{1,0:T(8,128)(2,1)S(1)}, bf16[256,768]{1,0:T(8,128)(2,1)S(1)}, u32[]{:S(2)}, u32[]{:S(2)}) collective-permute-start(bf16[256,768]{1,0:T(8,128)(2,1)S(1)} %get-tuple-element.32.refs_0_), channel_id=1, source_target_pairs={{0,16},{8,24},{16,0},{24,8},{1,17},{9,25},{17,1},{25,9},{2,18},{10... | collective-permute-start | bytes 1179656 | tf_op jit(solution)/shard_map/ppermute | solution.py:385
  85.9 11.8 %collective-permute-start.9 = (bf16[256,768]{1,0:T(8,128)(2,1)S(1)}, bf16[256,768]{1,0:T(8,128)(2,1)S(1)}, u32[]{:S(2)}, u32[]{:S(2)}) collective-permute-start(bf16[256,768]{1,0:T(8,128)(2,1)S(1)} %get-tuple-element.33), channel_id=1, source_target_pairs={{0,8},{8,0},{16,24},{24,16},{1,9},{9,1},{17,25},{25,17},{2,10},{10... | collective-permute-start | bytes 1179656 | tf_op jit(solution)/shard_map/ppermute | solution.py:382
  89.9 16.0 %collective-permute-start.12 = (bf16[256,768]{1,0:T(8,128)(2,1)S(1)}, bf16[256,768]{1,0:T(8,128)(2,1)S(1)}, u32[]{:S(2)}, u32[]{:S(2)}) collective-permute-start(bf16[256,768]{1,0:T(8,128)(2,1)S(1)} %get-tuple-element.38), channel_id=1, source_target_pairs={{0,16},{8,24},{16,0},{24,8},{1,17},{9,25},{17,1},{25,9},{2,18},{10... | collective-permute-start | bytes 1179656 | tf_op jit(solution)/shard_map/ppermute | solution.py:385
  97.4 8.4 %collective-permute-start.13 = (bf16[256,768]{1,0:T(8,128)(2,1)S(1)}, bf16[256,768]{1,0:T(8,128)(2,1)S(1)}, u32[]{:S(2)}, u32[]{:S(2)}) collective-permute-start(bf16[256,768]{1,0:T(8,128)(2,1)S(1)} %get-tuple-element.39), channel_id=1, source_target_pairs={{0,8},{8,0},{16,24},{24,16},{1,9},{9,1},{17,25},{25,17},{2,10},{10... | collective-permute-start | bytes 1179656 | tf_op jit(solution)/shard_map/ppermute | solution.py:382
  111.5 8.6 %collective-permute-start.16 = (bf16[8,256,768]{2,1,0:T(8,128)(2,1)}, bf16[8,256,768]{2,1,0:T(8,128)(2,1)S(1)}, u32[]{:S(2)}, u32[]{:S(2)}) collective-permute-start(bf16[8,256,768]{2,1,0:T(8,128)(2,1)} %get-tuple-element.41), channel_id=1, source_target_pairs={{0,1},{1,0},{2,3},{3,2},{4,5},{5,4},{6,7},{7,6},{8,9},{9,8},{10,11... | collective-permute-start | bytes 9437192 | tf_op jit(solution)/shard_map/ppermute | solution.py:388
  114.6 19.4 %collective-permute-start.14 = (bf16[2,256,768]{2,1,0:T(8,128)(2,1)}, bf16[2,256,768]{2,1,0:T(8,128)(2,1)}, u32[]{:S(2)}, u32[]{:S(2)}) collective-permute-start(bf16[2,256,768]{2,1,0:T(8,128)(2,1)} %get-tuple-element.40.s0.refs_0_.refs_1_), channel_id=1, source_target_pairs={{0,8},{8,0},{16,24},{24,16},{1,9},{9,1},{17,25},{25,17},{2,10},{10... | collective-permute-start | bytes 2359304 | tf_op jit(solution)/shard_map/ppermute | solution.py:382
  114.9 19.1 %collective-permute-start.15 = (bf16[2,256,768]{2,1,0:T(8,128)(2,1)}, bf16[2,256,768]{2,1,0:T(8,128)(2,1)}, u32[]{:S(2)}, u32[]{:S(2)}) collective-permute-start(bf16[2,256,768]{2,1,0:T(8,128)(2,1)} %get-tuple-element.40.s0.refs_0_.refs_1_), channel_id=1, source_target_pairs={{0,16},{8,24},{16,0},{24,8},{1,17},{9,25},{17,1},{25,9},{2,18},{10... | collective-permute-start | bytes 2359304 | tf_op jit(solution)/shard_map/ppermute | solution.py:385
  120.1 18.3 %copy-start = (bf16[8,256,768]{2,1,0:T(8,128)(2,1)}, bf16[8,256,768]{2,1,0:T(8,128)(2,1)S(1)}, u32[]{:S(2)}) copy-start(bf16[8,256,768]{2,1,0:T(8,128)(2,1)S(1)} %collective-permute-done.16.c1.s1.x1) | copy-start | bytes 9437188
  120.1 30.8 %collective-permute-start.20 = (bf16[2,256,768]{2,1,0:T(8,128)(2,1)}, bf16[2,256,768]{2,1,0:T(8,128)(2,1)}, u32[]{:S(2)}, u32[]{:S(2)}) collective-permute-start(bf16[2,256,768]{2,1,0:T(8,128)(2,1)} %get-tuple-element.44.s0), channel_id=1, source_target_pairs={{0,8},{8,0},{16,24},{24,16},{1,9},{9,1},{17,25},{25,17},{2,10},{10... | collective-permute-start | bytes 2359304 | tf_op jit(solution)/shard_map/ppermute | solution.py:382
  120.4 30.5 %collective-permute-start.21 = (bf16[2,256,768]{2,1,0:T(8,128)(2,1)}, bf16[2,256,768]{2,1,0:T(8,128)(2,1)}, u32[]{:S(2)}, u32[]{:S(2)}) collective-permute-start(bf16[2,256,768]{2,1,0:T(8,128)(2,1)} %get-tuple-element.44.s0), channel_id=1, source_target_pairs={{0,16},{8,24},{16,0},{24,8},{1,17},{9,25},{17,1},{25,9},{2,18},{10... | collective-permute-start | bytes 2359304 | tf_op jit(solution)/shard_map/ppermute | solution.py:385
  121.7 1.1 copy-start.6
  135.9 23.3 %collective-permute-start.18 = (bf16[256,768]{1,0:T(8,128)(2,1)S(1)}, bf16[256,768]{1,0:T(8,128)(2,1)}, u32[]{:S(2)}, u32[]{:S(2)}) collective-permute-start(bf16[256,768]{1,0:T(8,128)(2,1)S(1)} %get-tuple-element.42.rest_0_), channel_id=1, source_target_pairs={{0,16},{8,24},{16,0},{24,8},{1,17},{9,25},{17,1},{25,9},{2,18},{10... | collective-permute-start | bytes 1179656 | tf_op jit(solution)/shard_map/ppermute | solution.py:385
  137.2 22.1 %collective-permute-start.19 = (bf16[256,768]{1,0:T(8,128)(2,1)}, bf16[256,768]{1,0:T(8,128)(2,1)}, u32[]{:S(2)}, u32[]{:S(2)}) collective-permute-start(bf16[256,768]{1,0:T(8,128)(2,1)} %get-tuple-element.43), channel_id=1, source_target_pairs={{0,8},{8,0},{16,24},{24,16},{1,9},{9,1},{17,25},{25,17},{2,10},{10... | collective-permute-start | bytes 1179656 | tf_op jit(solution)/shard_map/ppermute | solution.py:382
  138.4 1.1 copy-start.3
  152.1 21.4 %copy-start.16 = (bf16[256,768]{1,0:T(8,128)(2,1)}, bf16[256,768]{1,0:T(8,128)(2,1)S(1)}, u32[]{:S(2)}) copy-start(bf16[256,768]{1,0:T(8,128)(2,1)S(1)} %get-tuple-element.47) | copy-start | bytes 1179652
  173.5 3.7 %copy-start.13 = (f32[4,64,1536]{2,1,0:T(8,128)}, f32[4,64,1536]{2,1,0:T(8,128)S(1)}, u32[]{:S(2)}) copy-start(f32[4,64,1536]{2,1,0:T(8,128)S(1)} %get-tuple-element.46) | copy-start | bytes 4718596
  173.5 18.1 %copy-start.7 = (bf16[256,1536]{1,0:T(8,128)(2,1)S(1)}, bf16[256,1536]{1,0:T(8,128)(2,1)}, u32[]{:S(2)}) copy-start(bf16[256,1536]{1,0:T(8,128)(2,1)} %copy-done.5) | copy-start | bytes 2359300
  173.5 5.7 %copy-start.17 = (bf16[256,768]{1,0:T(8,128)(2,1)S(1)}, bf16[256,768]{1,0:T(8,128)(2,1)}, u32[]{:S(2)}) copy-start(bf16[256,768]{1,0:T(8,128)(2,1)} %copy-done.16) | copy-start | bytes 1179652
  173.5 18.1 %collective-permute-start.28 = (bf16[6,256,768]{2,1,0:T(8,128)(2,1)}, bf16[6,256,768]{2,1,0:T(8,128)(2,1)}, u32[]{:S(2)}, u32[]{:S(2)}) collective-permute-start(bf16[6,256,768]{2,1,0:T(8,128)(2,1)} %get-tuple-element.48.s0), channel_id=1, source_target_pairs={{0,1},{1,0},{2,3},{3,2},{4,5},{5,4},{6,7},{7,6},{8,9},{9,8},{10,11... | collective-permute-start | bytes 7077896 | tf_op jit(solution)/shard_map/ppermute | solution.py:388
  177.2 40.7 %collective-permute-start.30 = (bf16[4,256,768]{2,1,0:T(8,128)(2,1)S(1)}, bf16[4,256,768]{2,1,0:T(8,128)(2,1)}, u32[]{:S(2)}, u32[]{:S(2)}) collective-permute-start(bf16[4,256,768]{2,1,0:T(8,128)(2,1)S(1)} %constant_dynamic-update-slice_fusion.rest_1_.s0), channel_id=1, source_target_pairs={{0,1},{1,0},{2,3},{3,2},{4,5},{5,4},{6,7},{7,6},{8,9},{9,8},{10,11... | collective-permute-start | bytes 4718600 | tf_op jit(solution)/shard_map/ppermute | solution.py:388
  177.8 10.7 %collective-permute-start.26 = (bf16[256,768]{1,0:T(8,128)(2,1)S(1)}, bf16[256,768]{1,0:T(8,128)(2,1)S(1)}, u32[]{:S(2)}, u32[]{:S(2)}) collective-permute-start(bf16[256,768]{1,0:T(8,128)(2,1)S(1)} %get-tuple-element.45.refs_9_.rest_2_), channel_id=1, source_target_pairs={{0,16},{8,24},{16,0},{24,8},{1,17},{9,25},{17,1},{25,9},{2,18},{10... | collective-permute-start | bytes 1179656 | tf_op jit(solution)/shard_map/ppermute | solution.py:385
  179.2 35.6 %collective-permute-start.27 = (bf16[256,768]{1,0:T(8,128)(2,1)S(1)}, bf16[256,768]{1,0:T(8,128)(2,1)S(1)}, u32[]{:S(2)}, u32[]{:S(2)}) collective-permute-start(bf16[256,768]{1,0:T(8,128)(2,1)S(1)} %copy-done.17), channel_id=1, source_target_pairs={{0,8},{8,0},{16,24},{24,16},{1,9},{9,1},{17,25},{25,17},{2,10},{10... | collective-permute-start | bytes 1179656 | tf_op jit(solution)/shard_map/ppermute | solution.py:382
  181.7 34.4 %collective-permute-start.25 = (bf16[1,64,1536]{2,1,0:T(8,128)(2,1)S(1)}, bf16[1,64,1536]{2,1,0:T(8,128)(2,1)S(1)}, u32[]{:S(2)}, u32[]{:S(2)}) collective-permute-start(bf16[1,64,1536]{2,1,0:T(8,128)(2,1)S(1)} %get-tuple-element.50), channel_id=1, source_target_pairs={{0,2},{2,4},{4,6},{6,0},{1,3},{3,5},{5,7},{7,1},{8,10},{10,12},{12... | collective-permute-start | bytes 589832 | tf_op jit(solution)/shard_map/ppermute | solution.py:391
  188.5 27.6 %collective-permute-start.24 = (bf16[1,64,1536]{2,1,0:T(8,128)(2,1)S(1)}, bf16[1,64,1536]{2,1,0:T(8,128)(2,1)S(1)}, u32[]{:S(2)}, u32[]{:S(2)}) collective-permute-start(bf16[1,64,1536]{2,1,0:T(8,128)(2,1)S(1)} %get-tuple-element.51), channel_id=1, source_target_pairs={{0,4},{2,6},{4,0},{6,2},{1,5},{3,7},{5,1},{7,3},{8,12},{10,14},{12... | collective-permute-start | bytes 589832 | tf_op jit(solution)/shard_map/ppermute | solution.py:391
  191.6 24.5 %collective-permute-start.23 = (bf16[1,64,1536]{2,1,0:T(8,128)(2,1)S(1)}, bf16[1,64,1536]{2,1,0:T(8,128)(2,1)S(1)}, u32[]{:S(2)}, u32[]{:S(2)}) collective-permute-start(bf16[1,64,1536]{2,1,0:T(8,128)(2,1)S(1)} %get-tuple-element.49), channel_id=1, source_target_pairs={{0,6},{2,0},{4,2},{6,4},{1,7},{3,1},{5,3},{7,5},{8,14},{10,8},{12,... | collective-permute-start | bytes 589832 | tf_op jit(solution)/shard_map/ppermute | solution.py:391
  191.6 1.7 copy-start.12
  214.8 3.1 %copy-start.4 = (bf16[256,1536]{1,0:T(8,128)(2,1)S(1)}, bf16[256,1536]{1,0:T(8,128)(2,1)}, u32[]{:S(2)}) copy-start(bf16[256,1536]{1,0:T(8,128)(2,1)} %copy-done.2) | copy-start | bytes 2359300
  214.8 19.1 %collective-permute-start.29 = (bf16[2,256,768]{2,1,0:T(8,128)(2,1)S(1)}, bf16[2,256,768]{2,1,0:T(8,128)(2,1)S(1)}, u32[]{:S(2)}, u32[]{:S(2)}) collective-permute-start(bf16[2,256,768]{2,1,0:T(8,128)(2,1)S(1)} %stack.1.rest_2_.s0), channel_id=1, source_target_pairs={{0,1},{1,0},{2,3},{3,2},{4,5},{5,4},{6,7},{7,6},{8,9},{9,8},{10,11... | collective-permute-start | bytes 2359304 | tf_op jit(solution)/shard_map/ppermute | solution.py:388
  217.9 16.1 %copy-start.1 = (bf16[8,256,768]{2,1,0:T(8,128)(2,1)S(1)}, bf16[8,256,768]{2,1,0:T(8,128)(2,1)}, u32[]{:S(2)}) copy-start(bf16[8,256,768]{2,1,0:T(8,128)(2,1)} %copy-done) | copy-start | bytes 9437188
  (1 other events, 0.9 us)
